TPU v7x, 32 devices: a whole 2x2x4 slice. The times are simulated.
32 devices in a mesh: ha: 8 (over y, x, core), wa: 4 (over z).
Axes of the slice: x: 2, y: 2, z: 4, core: 2. Of those that a mesh axis runs over, the one named last changes fastest.
Arguments:
- features: bfloat16 [7, 40, 80, 384], P(None, 'ha', 'wa'), may hold values from -6 to 6
- conv_weight: bfloat16 [10368, 384], P(('ha', 'wa')), may hold values from -0.0625 to 0.0625
- upconv_weight: bfloat16 [3456, 384], P(('ha', 'wa')), may hold values from -0.109375 to 0.109375
- norm_gain: bfloat16 [384], P(('ha', 'wa')), may hold values from 0.099609375 to 1.8984375
- cotangent: bfloat16 [5, 80, 160, 384], P(None, 'ha', 'wa'), may hold values from -6 to 6
Outputs:
- feature_grad: bfloat16 [7, 40, 80, 384], P(None, 'ha', 'wa')
- conv_grad: float32 [10368, 384], P(('ha', 'wa'))
- upconv_grad: float32 [3456, 384], P(('ha', 'wa'))
- gain_grad: float32 [384], P(('ha', 'wa'))
All inputs are finite; a program needn't handle non-finite values.
Results may differ from a plain program's by a relative error of at most 0.005.
Values may be sent and summed in bfloat16 or wider, within the bound.
A program may use at most 192 MiB of HBM per device.

v0:
```python
import math

import jax
import jax.numpy as jnp
from jax import lax
from jax.sharding import PartitionSpec as P

EPSILON = 1e-06


def padded_2(block, sides, width):
    for axis, dim in sides:
        count = lax.axis_size(axis)
        forward = [(i, i + 1) for i in range(count - 1)]
        backward = [(target, source) for source, target in forward]
        low = lax.ppermute(
            lax.slice_in_dim(block, block.shape[dim] - width, None, axis=dim), axis, forward
        )
        high = lax.ppermute(lax.slice_in_dim(block, 0, width, axis=dim), axis, backward)
        block = jnp.concatenate([low, block, high], axis=dim)
    return block


def tap_blocks(weight, channels, flipped):
    blocks = weight.reshape(-1, channels, channels)
    if flipped:
        blocks = jnp.swapaxes(blocks, 1, 2)
    return blocks


def flat_block(padded):
    frames_in, rows_in, cols_in, channels = padded.shape
    flat_rows = padded.reshape(frames_in * rows_in * cols_in, channels)
    return jnp.pad(flat_rows, ((0, 2 * cols_in + 2), (0, 0)))


def conv_taps(padded, blocks, out_frames, out_rows, out_cols, depth, flipped):
    frames_in, rows_in, cols_in, channels = padded.shape
    outputs = blocks.shape[-1]
    plane_size = rows_in * cols_in
    length = out_frames * plane_size
    flat_rows = flat_block(padded)
    total = jnp.zeros((length, outputs), jnp.float32)
    for time_tap in range(depth):
        for row_tap in range(3):
            for col_tap in range(3):
                index_tap = (time_tap * 3 + row_tap) * 3 + col_tap
                if flipped:
                    time_from, row_from, col_from = (depth - 1 - time_tap, 2 - row_tap, 2 - col_tap)
                else:
                    time_from, row_from, col_from = (time_tap, row_tap, col_tap)
                offset_rows = time_from * plane_size + row_from * cols_in + col_from
                window = lax.slice_in_dim(flat_rows, offset_rows, offset_rows + length, axis=0)
                total = total + jnp.dot(
                    window, blocks[index_tap], preferred_element_type=jnp.float32
                )
    return total.reshape(out_frames, rows_in, cols_in, outputs)[:, :out_rows, :out_cols]


def weight_grads(padded, cotan, out_frames, out_rows, out_cols, depth):
    frames_in, rows_in, cols_in, channels = padded.shape
    plane_size = rows_in * cols_in
    length = out_frames * plane_size
    flat_rows = flat_block(padded)
    placed = jnp.pad(cotan, ((0, 0), (0, rows_in - out_rows), (0, cols_in - out_cols), (0, 0)))
    flat_cot = placed.reshape(length, cotan.shape[-1])
    pieces = []
    for time_tap in range(depth):
        for row_tap in range(3):
            for col_tap in range(3):
                offset_rows = time_tap * plane_size + row_tap * cols_in + col_tap
                window = lax.slice_in_dim(flat_rows, offset_rows, offset_rows + length, axis=0)
                pieces.append(
                    lax.dot_general(
                        window,
                        flat_cot,
                        (((0,), (0,)), ((), ())),
                        preferred_element_type=jnp.float32,
                    )
                )
    return jnp.concatenate(pieces, axis=0)


def norm_parts(hidden, gain):
    inverse = lax.rsqrt(jnp.mean(hidden * hidden, axis=-1, keepdims=True) + EPSILON)
    return (inverse, hidden * inverse * gain.astype(jnp.float32))


def norm_backward(hidden, inverse, normed, gain, grad_act):
    sigmoid_v = jax.nn.sigmoid(normed)
    grad_norm = grad_act * sigmoid_v * (1.0 + normed * (1.0 - sigmoid_v))
    gain_terms = jnp.sum(grad_norm * hidden * inverse, axis=(0, 1, 2))
    grad_q = grad_norm * gain.astype(jnp.float32)
    centre = jnp.mean(grad_q * hidden, axis=-1, keepdims=True)
    grad_hidden = (inverse * (grad_q - hidden * inverse * inverse * centre)).astype(jnp.bfloat16)
    return (grad_hidden, gain_terms)


def upsample(active):
    frames, height, breadth, channels = active.shape
    spread = jnp.broadcast_to(
        active[:, :, None, :, None, :], (frames, height, 2, breadth, 2, channels)
    )
    return spread.reshape(frames, 2 * height, 2 * breadth, channels)


def body(features, conv_weight, upconv_weight, norm_gain, cotangent):
    frames = cotangent.shape[0]
    height = features.shape[1]
    breadth = features.shape[2]
    channels = features.shape[3]
    grid_rows = height * lax.axis_size("ha")
    grid_cols = breadth * lax.axis_size("wa")
    factor = 1.0 / math.sqrt(frames * grid_rows * grid_cols)
    first, second, gain = (
        lax.all_gather(conv_weight, ("ha", "wa"), axis=0, tiled=True),
        lax.all_gather(upconv_weight, ("ha", "wa"), axis=0, tiled=True),
        lax.all_gather(norm_gain, ("ha", "wa"), axis=0, tiled=True),
    )
    wide = padded_2(features, (("ha", 1), ("wa", 2)), 2)
    hidden_ext = conv_taps(
        wide, tap_blocks(first, channels, False), frames, height + 2, breadth + 2, 3, False
    )
    inverse_ext, normed_ext = norm_parts(hidden_ext, gain)
    row_ids = lax.axis_index("ha") * height + lax.iota(jnp.int32, height + 2) - 1
    col_ids = lax.axis_index("wa") * breadth + lax.iota(jnp.int32, breadth + 2) - 1
    inside = ((row_ids >= 0) & (row_ids < grid_rows))[:, None] & (
        (col_ids >= 0) & (col_ids < grid_cols)
    )[None, :]
    active = jnp.where(inside[None, :, :, None], jax.nn.silu(normed_ext), 0.0).astype(jnp.bfloat16)
    upsampled = upsample(active)[:, 1:-1, 1:-1]
    cot_wide = padded_2(cotangent, (("ha", 1), ("wa", 2)), 1)
    grad_up = conv_taps(
        cot_wide, tap_blocks(second, channels, True), frames, 2 * height, 2 * breadth, 1, True
    )
    grad_act = grad_up.reshape(frames, height, 2, breadth, 2, channels).sum(axis=(2, 4))
    hidden = hidden_ext[:, 1:-1, 1:-1]
    inverse = inverse_ext[:, 1:-1, 1:-1]
    normed = normed_ext[:, 1:-1, 1:-1]
    grad_hidden, gain_terms = norm_backward(hidden, inverse, normed, gain, grad_act)
    flipped_first = tap_blocks(first, channels, True)
    grad_wide = padded_2(grad_hidden, (("ha", 1), ("wa", 2)), 1)
    grad_wide = jnp.pad(grad_wide, ((2, 2), (0, 0), (0, 0), (0, 0)))
    grad_feat = conv_taps(grad_wide, flipped_first, frames + 2, height, breadth, 3, True)
    feature_grad = grad_feat.astype(jnp.bfloat16)
    local_first = (
        weight_grads(wide[:, 1:-1, 1:-1], grad_hidden, frames, height, breadth, 3) * factor
    )
    local_second = weight_grads(upsampled, cotangent, frames, 2 * height, 2 * breadth, 1) * (
        0.5 * factor
    )
    local_gain = gain_terms * factor
    part_first, part_second, part_gain = (
        lax.psum_scatter(local_first, "ha", scatter_dimension=0, tiled=True),
        lax.psum_scatter(local_second, "ha", scatter_dimension=0, tiled=True),
        lax.psum_scatter(local_gain, "ha", scatter_dimension=0, tiled=True),
    )
    conv_grad, upconv_grad, gain_grad = (
        lax.psum_scatter(part_first, "wa", scatter_dimension=0, tiled=True),
        lax.psum_scatter(part_second, "wa", scatter_dimension=0, tiled=True),
        lax.psum_scatter(part_gain, "wa", scatter_dimension=0, tiled=True),
    )
    return (feature_grad, conv_grad, upconv_grad, gain_grad)


def solution(mesh):
    return jax.shard_map(
        body,
        mesh=mesh,
        in_specs=(
            P(None, "ha", "wa", None),
            P(("ha", "wa"), None),
            P(("ha", "wa"), None),
            P(("ha", "wa")),
            P(None, "ha", "wa", None),
        ),
        out_specs=(
            P(None, "ha", "wa", None),
            P(("ha", "wa"), None),
            P(("ha", "wa"), None),
            P(("ha", "wa")),
        ),
        check_vma=False,
    )
```

profile of v0, /device:TPU:0, one launch (start us, length us, event | category | flops | bytes accessed | tf_op | source)
XLA Modules:
  0.0 490.6 jit_solution(12799703200269238036)
XLA Ops:
  15.4 5.8 %collective-permute-start.4 = (bf16[5,1,40,384]{3,2,1,0:T(8,128)(2,1)}, bf16[5,1,40,384]{3,2,1,0:T(8,128)(2,1)}, u32[]{:S(2)}, u32[]{:S(2)}) collective-permute-start(bf16[5,1,40,384]{3,2,1,0:T(8,128)(2,1)} %get-tuple-element.16), channel_id=1, source_target_pairs={{0,4},{4,8},{8,12},{12,16},{16,20},{20,24},{24,28},{1,5},{5,9},{9,... | collective-permute-start | bytes 460808 | tf_op jit(solution)/shard_map/ppermute | solution.py:16
  24.6 43.7 %all-reduce.8 = bf16[384]{0:T(512)(128)(2,1)} all-reduce(bf16[384]{0:T(512)(128)(2,1)} %dynamic-update-slice), channel_id=1, replica_groups=mesh['ha'=8,'wa'=4] {'ha','wa'}, use_global_device_ids=true, to_apply=%add.8 | all-reduce | flops 384 | bytes 1536
  76.6 4.6 collective-permute-start.6
  83.9 4.6 collective-permute-start.2
  100.9 4.4 reshape.192
  117.6 14.2 %convolution_add_fusion.1 = f32[2520,384]{1,0:T(8,128)S(1)} fusion(f32[2520,384]{1,0:T(8,128)S(1)} %convolution_add_fusion.2, bf16[2520,384]{1,0:T(8,128)(2,1)S(1)} %reshape.191, bf16[9,384,384]{1,2,0:T(8,128)(2,1)S(1)} %bitcast.257), kind=kOutput, calls=%fused_computation.2 | convolution fusion | flops 744145920 | bytes 9971712 | tf_op jit(solution)/shard_map/dot_general | solution.py:54
  131.8 3.6 convolution_add_fusion
  135.4 4.9 reshape.193
  140.3 3.7 slice.901
  144.0 5.0 %reshape.194 = f32[5,5,2,20,2,384]{5,4,3,2,1,0:T(2,128)} reshape(f32[5,10,40,384]{3,2,1,0:T(8,128)} %slice.901) | data formatting | bytes 6144000 | tf_op jit(solution)/shard_map/reshape | solution.py:136
  149.0 4.0 reduce_sum.37
  153.1 9.2 %reshape.206 = bf16[10368,384]{1,0:T(8,128)(2,1)} reshape(bf16[32,324,384]{2,1,0:T(8,128)(2,1)} %all-gather.5.cloned.1.call-done) | data formatting | bytes 15925248
  193.0 4.8 reshape.200
  197.8 4.4 fusion.56
  220.1 4.4 fusion.29
  239.0 5.3 %broadcast_multiply_fusion.1 = f32[3456,384]{1,0:T(8,128)} fusion(f32[3456,384]{1,0:T(8,128)} %fusion.50), kind=kLoop, calls=%fused_computation.64 | loop fusion | flops 1327104 | bytes 10616832 | tf_op jit(solution)/shard_map/mul | solution.py:149
  270.9 11.1 %broadcast_multiply_fusion = f32[10368,384]{1,0:T(8,128)} fusion(f32[10368,384]{1,0:T(8,128)} %convolution_dynamic-update-slice_fusion), kind=kLoop, calls=%fused_computation | loop fusion | flops 3981312 | bytes 31850496 | tf_op jit(solution)/shard_map/mul | solution.py:147
  291.6 4.5 collective-permute-start.10
  296.2 14.3 %all-reduce.11 = f32[384]{0:T(512)S(1)} all-reduce(f32[384]{0:T(512)S(1)} %broadcast_multiply_fusion.3), channel_id=6, replica_groups=mesh['ha'=8,'wa'=4] {'ha'}, use_global_device_ids=true, to_apply=%region_8.9.clone | all-reduce | flops 384 | bytes 3072
  310.6 9.3 %all-reduce.12 = f32[48]{0:T(128)S(1)} all-reduce(f32[48]{0:T(128)S(1)} %dynamic-slice.5), channel_id=7, replica_groups=mesh['ha'=8,'wa'=4] {'wa'}, use_global_device_ids=true, to_apply=%region_9.10.clone | all-reduce | flops 48 | bytes 384
  320.5 10.1 %reshape.196 = bf16[27,384,384]{2,1,0:T(8,128)(2,1)} reshape(bf16[32,324,384]{2,1,0:T(8,128)(2,1)} %all-gather.5.cloned.1.call-done) | data formatting | bytes 15925248 | tf_op jit(solution)/shard_map/reshape | solution.py:25
  362.8 56.3 %reduce-scatter.7.cloned.1.call-done = f32[1296,384]{1,0:T(8,128)} async-done(((f32[10368,384]{1,0:T(8,128)}), f32[1296,384]{1,0:T(8,128)}) %reduce-scatter.7.cloned.1.call-update) | async-done | bytes 1990672 | tf_op jit(solution)/shard_map/reduce_scatter | solution.py:154
  419.1 51.4 %fusion.256 = (f32[336,384]{1,0:T(8,128)S(1)}, f32[112,384]{1,0:T(8,128)S(1)}) fusion(f32[1296,384]{1,0:T(8,128)} %reduce-scatter.7.cloned.1.call-done, f32[432,384]{1,0:T(8,128)} %reduce-scatter.9.cloned.1.call-done), kind=kCustom, calls=%all-reduce-scatter.2 | all-reduce-scatter fusion | flops 688130 | bytes 3342848
  470.5 3.3 collective-permute-start.13
  (244 shorter events, 186.2 us)
Async XLA Ops:
  7.2 93.7 %all-gather.7.cloned.1.call-start = ((), (), s32[]{:S(2)}) async-start(), calls=%async_computation.5 | async-start | bytes 2838528 | tf_op jit(solution)/shard_map/all_gather | solution.py:117
  7.9 145.1 %all-gather.5.cloned.1.call-start = ((), (), s32[]{:S(2)}) async-start(), calls=%async_computation.4 | async-start | bytes 8312832 | tf_op jit(solution)/shard_map/all_gather | solution.py:116
  8.6 354.2 %reduce-scatter.9.cloned.1.call-start = ((), (), s32[]{:S(2)}) async-start(), calls=%async_computation.3 | async-start | bytes 5971968 | tf_op jit(solution)/shard_map/reduce_scatter | solution.py:155
  8.7 13.8 %copy-start.5 = (bf16[5,10,40,384]{3,2,1,0:T(8,128)(2,1)S(1)}, bf16[5,10,40,384]{3,2,1,0:T(8,128)(2,1)}, u32[]{:S(2)}) copy-start(bf16[5,10,40,384]{3,2,1,0:T(8,128)(2,1)} %param.9) | copy-start | bytes 4608004
  10.0 71.1 %collective-permute-start = (bf16[7,2,20,384]{3,2,1,0:T(8,128)(2,1)S(1)}, bf16[7,2,20,384]{3,2,1,0:T(8,128)(2,1)S(1)}, u32[]{:S(2)}, u32[]{:S(2)}) collective-permute-start(bf16[7,2,20,384]{3,2,1,0:T(8,128)(2,1)S(1)} %copy.27), channel_id=1, source_target_pairs={{0,4},{4,8},{8,12},{12,16},{16,20},{20,24},{24,28},{1,5},{5,9},{9,... | collective-permute-start | bytes 645128 | tf_op jit(solution)/shard_map/ppermute | solution.py:16
  12.4 68.9 %collective-permute-start.1 = (bf16[7,2,20,384]{3,2,1,0:T(8,128)(2,1)S(1)}, bf16[7,2,20,384]{3,2,1,0:T(8,128)(2,1)S(1)}, u32[]{:S(2)}, u32[]{:S(2)}) collective-permute-start(bf16[7,2,20,384]{3,2,1,0:T(8,128)(2,1)S(1)} %copy.28), channel_id=1, source_target_pairs={{4,0},{8,4},{12,8},{16,12},{20,16},{24,20},{28,24},{5,1},{9,5},{13... | collective-permute-start | bytes 645128 | tf_op jit(solution)/shard_map/ppermute | solution.py:19
  15.4 57.0 %collective-permute-start.4 = (bf16[5,1,40,384]{3,2,1,0:T(8,128)(2,1)}, bf16[5,1,40,384]{3,2,1,0:T(8,128)(2,1)}, u32[]{:S(2)}, u32[]{:S(2)}) collective-permute-start(bf16[5,1,40,384]{3,2,1,0:T(8,128)(2,1)} %get-tuple-element.16), channel_id=1, source_target_pairs={{0,4},{4,8},{8,12},{12,16},{16,20},{20,24},{24,28},{1,5},{5,9},{9,... | collective-permute-start | bytes 460808 | tf_op jit(solution)/shard_map/ppermute | solution.py:16
  21.2 53.9 %collective-permute-start.5 = (bf16[5,1,40,384]{3,2,1,0:T(8,128)(2,1)S(1)}, bf16[5,1,40,384]{3,2,1,0:T(8,128)(2,1)S(1)}, u32[]{:S(2)}, u32[]{:S(2)}) collective-permute-start(bf16[5,1,40,384]{3,2,1,0:T(8,128)(2,1)S(1)} %get-tuple-element.15), channel_id=1, source_target_pairs={{4,0},{8,4},{12,8},{16,12},{20,16},{24,20},{28,24},{5,1},{9,5},{13... | collective-permute-start | bytes 460808 | tf_op jit(solution)/shard_map/ppermute | solution.py:19
  73.3 7.9 %copy-start.14 = (bf16[7,5,20,384]{3,0,2,1:T(8,128)(2,1)S(1)}, bf16[7,5,20,384]{3,0,2,1:T(8,128)(2,1)}, u32[]{:S(2)}) copy-start(bf16[7,5,20,384]{3,0,2,1:T(8,128)(2,1)} %param.5) | copy-start | bytes 1612804
  75.3 13.2 %collective-permute-start.7 = (bf16[5,12,1,384]{3,2,1,0:T(2,128)(2,1)S(1)}, bf16[5,12,1,384]{3,2,1,0:T(2,128)(2,1)S(1)}, u32[]{:S(2)}, u32[]{:S(2)}) collective-permute-start(bf16[5,12,1,384]{3,2,1,0:T(2,128)(2,1)S(1)} %get-tuple-element.14), channel_id=1, source_target_pairs={{1,0},{2,1},{3,2},{5,4},{6,5},{7,6},{9,8},{10,9},{11,10},{13,12},{... | collective-permute-start | bytes 138248 | tf_op jit(solution)/shard_map/ppermute | solution.py:19
  76.6 11.9 %collective-permute-start.6 = (bf16[5,12,1,384]{3,2,1,0:T(2,128)(2,1)S(1)}, bf16[5,12,1,384]{3,2,1,0:T(2,128)(2,1)S(1)}, u32[]{:S(2)}, u32[]{:S(2)}) collective-permute-start(bf16[5,12,1,384]{3,2,1,0:T(2,128)(2,1)S(1)} %get-tuple-element.13), channel_id=1, source_target_pairs={{0,1},{1,2},{2,3},{4,5},{5,6},{6,7},{8,9},{9,10},{10,11},{12,13},{... | collective-permute-start | bytes 138248 | tf_op jit(solution)/shard_map/ppermute | solution.py:16
  82.6 11.2 %collective-permute-start.3 = (bf16[7,9,2,384]{3,2,1,0:T(2,128)(2,1)S(1)}, bf16[7,9,2,384]{3,2,1,0:T(2,128)(2,1)S(1)}, u32[]{:S(2)}, u32[]{:S(2)}) collective-permute-start(bf16[7,9,2,384]{3,2,1,0:T(2,128)(2,1)S(1)} %get-tuple-element.24), channel_id=1, source_target_pairs={{1,0},{2,1},{3,2},{5,4},{6,5},{7,6},{9,8},{10,9},{11,10},{13,12},{... | collective-permute-start | bytes 290312 | tf_op jit(solution)/shard_map/ppermute | solution.py:19
  83.9 9.9 %collective-permute-start.2 = (bf16[7,9,2,384]{3,2,1,0:T(2,128)(2,1)S(1)}, bf16[7,9,2,384]{3,2,1,0:T(2,128)(2,1)S(1)}, u32[]{:S(2)}, u32[]{:S(2)}) collective-permute-start(bf16[7,9,2,384]{3,2,1,0:T(2,128)(2,1)S(1)} %get-tuple-element.23), channel_id=1, source_target_pairs={{0,1},{1,2},{2,3},{4,5},{5,6},{6,7},{8,9},{9,10},{10,11},{12,13},{... | collective-permute-start | bytes 290312 | tf_op jit(solution)/shard_map/ppermute | solution.py:16
  244.3 174.8 %reduce-scatter.7.cloned.1.call-start = ((), (), s32[]{:S(2)}) async-start(), calls=%async_computation.2 | async-start | bytes 17915904 | tf_op jit(solution)/shard_map/reduce_scatter | solution.py:154
  282.0 4.4 copy-start.23
  282.0 6.3 %copy-start.24 = (u32[32]{0:T(128)S(1)}, u32[32]{0:T(128)}, u32[]{:S(2)}) copy-start(u32[32]{0:T(128)} %constant.81) | copy-start | bytes 388
  282.0 8.2 %collective-permute-start.9 = (bf16[5,1,20,384]{3,2,1,0:T(8,128)(2,1)S(1)}, bf16[5,1,20,384]{3,2,1,0:T(8,128)(2,1)S(1)}, u32[]{:S(2)}, u32[]{:S(2)}) collective-permute-start(bf16[5,1,20,384]{3,2,1,0:T(8,128)(2,1)S(1)} %get-tuple-element.30), channel_id=1, source_target_pairs={{4,0},{8,4},{12,8},{16,12},{20,16},{24,20},{28,24},{5,1},{9,5},{13... | collective-permute-start | bytes 230408 | tf_op jit(solution)/shard_map/ppermute | solution.py:19
  283.3 6.9 %collective-permute-start.8 = (bf16[5,1,20,384]{3,2,1,0:T(8,128)(2,1)S(1)}, bf16[5,1,20,384]{3,2,1,0:T(8,128)(2,1)S(1)}, u32[]{:S(2)}, u32[]{:S(2)}) collective-permute-start(bf16[5,1,20,384]{3,2,1,0:T(8,128)(2,1)S(1)} %get-tuple-element.29), channel_id=1, source_target_pairs={{0,4},{4,8},{8,12},{12,16},{16,20},{20,24},{24,28},{1,5},{5,9},{9,... | collective-permute-start | bytes 230408 | tf_op jit(solution)/shard_map/ppermute | solution.py:16
  290.3 40.3 %collective-permute-start.11 = (bf16[5,7,1,384]{3,2,1,0:T(2,128)(2,1)S(1)}, bf16[5,7,1,384]{3,2,1,0:T(2,128)(2,1)S(1)}, u32[]{:S(2)}, u32[]{:S(2)}) collective-permute-start(bf16[5,7,1,384]{3,2,1,0:T(2,128)(2,1)S(1)} %get-tuple-element.26), channel_id=1, source_target_pairs={{1,0},{2,1},{3,2},{5,4},{6,5},{7,6},{9,8},{10,9},{11,10},{13,12},{... | collective-permute-start | bytes 80648 | tf_op jit(solution)/shard_map/ppermute | solution.py:19
  291.6 39.0 %collective-permute-start.10 = (bf16[5,7,1,384]{3,2,1,0:T(2,128)(2,1)S(1)}, bf16[5,7,1,384]{3,2,1,0:T(2,128)(2,1)S(1)}, u32[]{:S(2)}, u32[]{:S(2)}) collective-permute-start(bf16[5,7,1,384]{3,2,1,0:T(2,128)(2,1)S(1)} %get-tuple-element.25), channel_id=1, source_target_pairs={{0,1},{1,2},{2,3},{4,5},{5,6},{6,7},{8,9},{9,10},{10,11},{12,13},{... | collective-permute-start | bytes 80648 | tf_op jit(solution)/shard_map/ppermute | solution.py:16
  337.4 7.3 %slice-start = ((s8[7962624]{0:T(1024)(128)(4,1)}), s8[4194304]{0:T(1024)(128)(4,1)S(1)}, s32[]{:S(2)}) async-start(s8[7962624]{0:T(1024)(128)(4,1)} %bitcast.222), calls=%async_computation.6 | async-start | bytes 8388608
  362.8 111.0 %copy-start.7 = (bf16[1078,384]{1,0:T(8,128)(2,1)S(1)}, bf16[1078,384]{1,0:T(8,128)(2,1)}, u32[]{:S(2)}) copy-start(bf16[1078,384]{1,0:T(8,128)(2,1)} %slice.798) | copy-start | bytes 2483716
  470.5 10.2 %collective-permute-start.13 = (f32[12,384]{1,0:T(8,128)S(1)}, f32[12,384]{1,0:T(8,128)S(1)}, u32[]{:S(2)}, u32[]{:S(2)}) collective-permute-start(f32[12,384]{1,0:T(8,128)S(1)} %slice.975), channel_id=1, source_target_pairs={{0,1},{1,2},{2,3},{4,5},{5,6},{6,7},{8,9},{9,10},{10,11},{12,13},{... | collective-permute-start | bytes 55304
  478.8 3.8 collective-permute-start.12
  (21 other events, 48.5 us)
Sparse Core Ops, SparseCore 0:
  10.8 61.1 all-gather.6
  74.8 75.6 all-gather.4
  244.4 57.8 reduce-scatter.8
  306.2 112.8 reduce-scatter.6
where the time goes:
time: 496 us; the launch traced here: 491 us
  matrix products  145 us (29%)
  blocking collectives  119 us (24%)
  local copies, waits for them, and re-layouts  82.8 us (17%)
  waiting for transfers between devices  58.6 us (12%)
  starting transfers between devices  38.4 us (8%)
  other arithmetic  29.5 us (6%)
  between operations  17.7 us (4%)
    unnamed x4, blocking collectives  119 us
    dot_general x63, matrix products, conv_taps(): jnp.dot(window, blocks[index_tap], preferred_element_type=jnp.float32)  82 us
    dot_general x36, matrix products, weight_grads(): lax.dot_general(window, flat_cot, (((0,), (0,)), ((), ())), preferred_ele...  62.9 us
    reduce_scatter x1, waiting for transfers between devices, body(): lax.psum_scatter(local_first, 'ha', scatter_dimension=0, tiled=True)  56.3 us
    ppermute x6, starting transfers between devices, padded_2(): lax.ppermute(lax.slice_in_dim(block, block.shape[dim] - width, None, axis...  24.9 us
    unnamed x74, local copies, waits for them, and re-layouts  21.5 us
    reshape x2, local copies, waits for them, and re-layouts, tap_blocks(): blocks = weight.reshape(-1, channels, channels)  14.5 us
    mul x1, other arithmetic, body(): weight_grads(wide[:, 1:-1, 1:-1], grad_hidden, frames, height, breadth, 3)  11.1 us
  transfers between devices with their start and end apart: 18, of which 2 were waited for; matrix products, arithmetic and copies ran while one was open for 33% of the time, Pallas kernels for 0%

commit v1 on v0

v1 whole, which is shorter than its diff:
```python
import math

import jax
import jax.numpy as jnp
from jax import lax
from jax.sharding import PartitionSpec as P

EPSILON = 1e-06


def with_halo(block, sides):
    for axis, dim in sides:
        count = lax.axis_size(axis)
        forward = [(i, i + 1) for i in range(count - 1)]
        backward = [(target, source) for source, target in forward]
        low = lax.ppermute(
            lax.slice_in_dim(block, block.shape[dim] - 1, None, axis=dim), axis, forward
        )
        high = lax.ppermute(lax.slice_in_dim(block, 0, 1, axis=dim), axis, backward)
        block = jnp.concatenate([low, block, high], axis=dim)
    return block


def flat_cells(window, plane):
    frames, height, breadth, channels = window.shape
    cells = window.reshape(frames, height * breadth, channels)
    return jnp.pad(cells, ((0, 0), (0, plane - height * breadth), (0, 0)))


def spatial_taps(wide, height, breadth, plane, flipped):
    pieces = []
    for row_tap in range(3):
        for col_tap in range(3):
            b, c = (2 - row_tap, 2 - col_tap) if flipped else (row_tap, col_tap)
            pieces.append(flat_cells(wide[:, b : b + height, c : c + breadth], plane))
    return jnp.concatenate(pieces, axis=-1)


def halve(block, axis, bits, left):
    count = lax.axis_size(axis)
    me = lax.axis_index(axis)
    left = list(left)
    for bit in bits:
        place = left.index(bit)
        mine = (me >> bit) & 1
        send = lax.dynamic_index_in_dim(block, 1 - mine, place, keepdims=False)
        keep = lax.dynamic_index_in_dim(block, mine, place, keepdims=False)
        got = lax.ppermute(
            send.astype(jnp.bfloat16), axis, [(i, i ^ (1 << bit)) for i in range(count)]
        )
        block = keep.astype(jnp.float32) + got.astype(jnp.float32)
        left.remove(bit)
    return block


def bits_of(count):
    return list(range(count.bit_length() - 1))


def body(features, conv_weight, upconv_weight, norm_gain, cotangent):
    f32, bf16 = jnp.float32, jnp.bfloat16
    frames = cotangent.shape[0]
    frames_in, height, breadth, channels = features.shape
    n_ha, n_wa = lax.axis_size("ha"), lax.axis_size("wa")
    cells = height * breadth
    plane = -(-cells // 16) * 16
    factor = 1.0 / math.sqrt(frames * cells * n_ha * n_wa)
    ha_bits, wa_bits = bits_of(n_ha), bits_of(n_wa)
    own_gain = norm_gain.shape[0]
    up_rows = upconv_weight.shape[0]
    sides = (("ha", 1), ("wa", 2))

    gain_row = jnp.pad(norm_gain[None, :], ((0, 3), (0, channels - own_gain)))
    packed = lax.all_gather(
        jnp.concatenate([upconv_weight, gain_row], axis=0), ("ha", "wa"), axis=0, tiled=False
    )
    second = packed[:, :up_rows].reshape(3, 3, channels, channels).astype(f32)
    gain = packed[:, up_rows, :own_gain].reshape(channels).astype(f32)
    first = lax.all_gather(conv_weight, ("ha", "wa"), axis=0, tiled=True)

    cot_wide = with_halo(cotangent, sides)
    pairs = cot_wide.reshape(frames, height + 1, 2, breadth + 1, 2 * channels)
    pieces = []
    for d in range(4):
        for off in range(2):
            window = pairs[:, d // 2 : d // 2 + height, d % 2, off : off + breadth]
            pieces.append(flat_cells(window, plane))
    cot_taps = jnp.concatenate(pieces, axis=-1).reshape(frames * plane, 16 * channels)
    turned = jnp.swapaxes(second, 2, 3)
    rows = [turned[2], turned[1] + turned[2], turned[0] + turned[1], turned[0]]
    mixed = [
        jnp.stack([row[2], row[1] + row[2], row[0] + row[1], row[0]]) for row in rows
    ]
    mixed = jnp.stack(mixed).astype(bf16).reshape(16 * channels, channels)
    grad_act = jnp.dot(cot_taps, mixed, preferred_element_type=f32)

    wide = with_halo(features, sides)
    taps = spatial_taps(wide, height, breadth, plane, False).reshape(
        frames_in * plane, 9 * channels
    )
    size = 9 * channels
    length = frames * plane
    hidden = jnp.zeros((length, channels), f32)
    for a in range(3):
        hidden = hidden + jnp.dot(
            taps[a * plane : a * plane + length],
            first[a * size : (a + 1) * size],
            preferred_element_type=f32,
        )

    inverse = lax.rsqrt(jnp.mean(hidden * hidden, axis=-1, keepdims=True) + EPSILON)
    normed = hidden * inverse * gain
    sigmoid_v = jax.nn.sigmoid(normed)
    active = (normed * sigmoid_v).astype(bf16)
    grad_norm = grad_act * sigmoid_v * (1.0 + normed * (1.0 - sigmoid_v))
    gain_terms = jnp.sum(grad_norm * hidden * inverse, axis=0)
    grad_q = grad_norm * gain
    centre = jnp.mean(grad_q * hidden, axis=-1, keepdims=True)
    grad_hidden = (inverse * (grad_q - hidden * inverse * inverse * centre)).astype(bf16)

    over_rows = (((0,), (0,)), ((), ()))
    local_first = jnp.concatenate(
        [
            (
                lax.dot_general(
                    taps[a * plane : a * plane + length],
                    grad_hidden,
                    over_rows,
                    preferred_element_type=f32,
                )
                * factor
            ).astype(bf16)
            for a in range(3)
        ],
        axis=0,
    )
    cross = lax.dot_general(active, cot_taps, over_rows, preferred_element_type=f32)
    cross = [
        [cross[:, (4 * d + e) * channels : (4 * d + e + 1) * channels] for e in range(4)]
        for d in range(4)
    ]
    local_second = jnp.concatenate(
        [
            (
                (
                    cross[2 - b][2 - c]
                    + cross[2 - b][3 - c]
                    + cross[3 - b][2 - c]
                    + cross[3 - b][3 - c]
                )
                * (0.5 * factor)
            ).astype(bf16)
            for b in range(3)
            for c in range(3)
        ],
        axis=0,
    )
    up_part = local_second.shape[0] // n_ha
    gain_rows = -(-n_wa // 16) * 16
    gain_part = jnp.pad(
        (gain_terms * factor).astype(bf16).reshape(n_ha, n_wa, own_gain),
        ((0, 0), (0, gain_rows - n_wa), (0, channels - own_gain)),
    )
    small = jnp.concatenate([local_second.reshape(n_ha, up_part, channels), gain_part], axis=1)
    small = small.reshape((2,) * len(ha_bits) + small.shape[1:])
    small = halve(small, "ha", ha_bits, ha_bits[::-1])
    ups = small[:up_part].reshape(n_wa, up_rows, channels)
    small = jnp.concatenate([ups, small[up_part : up_part + n_wa][:, None]], axis=1)
    small = small.reshape((2,) * len(wa_bits) + small.shape[1:])
    small = halve(small, "wa", wa_bits, wa_bits[::-1])
    upconv_grad = small[:up_rows]
    gain_grad = small[up_rows, :own_gain]

    part = local_first.shape[0] // n_ha
    big = local_first.reshape((2,) * len(ha_bits) + (part, channels))
    big = halve(big, "ha", [0], ha_bits[::-1])
    left = ha_bits[:0:-1]
    ends = []
    for side, order in ((0, ha_bits[1:]), (1, left)):
        half = big[..., side * part // 2 : (side + 1) * part // 2, :]
        ends.append(halve(half, "ha", order, left))
    big = jnp.stack(ends).reshape((2,) * len(wa_bits) + (part // n_wa, channels))
    conv_grad = halve(big, "wa", wa_bits, wa_bits[::-1])

    grad_wide = with_halo(
        grad_hidden.reshape(frames, plane, channels)[:, :cells].reshape(
            frames, height, breadth, channels
        ),
        sides,
    )
    grad_taps = spatial_taps(grad_wide, height, breadth, plane, True)
    grad_taps = jnp.pad(grad_taps, ((2, 2), (0, 0), (0, 0))).reshape((frames + 4) * plane, size)
    turned = jnp.swapaxes(first.reshape(3, 9, channels, channels), 2, 3).reshape(3, size, channels)
    long = (frames + 2) * plane
    feature = jnp.zeros((long, channels), f32)
    for a in range(3):
        start = (2 - a) * plane
        feature = feature + jnp.dot(
            grad_taps[start : start + long], turned[a], preferred_element_type=f32
        )
    feature_grad = (
        feature.astype(bf16)
        .reshape(frames + 2, plane, channels)[:, :cells]
        .reshape(frames + 2, height, breadth, channels)
    )
    return (feature_grad, conv_grad, upconv_grad, gain_grad)


def solution(mesh):
    return jax.shard_map(
        body,
        mesh=mesh,
        in_specs=(
            P(None, "ha", "wa", None),
            P(("ha", "wa"), None),
            P(("ha", "wa"), None),
            P(("ha", "wa")),
            P(None, "ha", "wa", None),
        ),
        out_specs=(
            P(None, "ha", "wa", None),
            P(("ha", "wa"), None),
            P(("ha", "wa"), None),
            P(("ha", "wa")),
        ),
        check_vma=False,
    )
```

time: 496 us -> 378 us (0.76)
  blocking collectives: 119 us -> 0 us
  matrix products: 145 us -> 50.2 us
  local copies, waits for them, and re-layouts: 82.8 us -> 127 us
  waiting for transfers between devices: 58.6 us -> 81.8 us
  other arithmetic: 29.5 us -> 48.5 us
  starting transfers between devices: 38.4 us -> 50 us
    unnamed x4 -> x0, blocking collectives: 119 us -> none
    dot_general x99 -> x11, matrix products: 145 us -> 50.2 us  [the longest x3 14 us: body(): jnp.dot(grad_taps[start:start + long], turned[a], preferred_element_type=...]
    reduce_scatter x2 -> x0, waiting for transfers between devices: 56.3 us -> none  [the longest x1 56.3 us: body(): lax.psum_scatter(local_first, 'ha', scatter_dimension=0, tiled=True)]
    ppermute x12 -> x24, waiting for transfers between devices: 0.03 us -> 43.3 us  [the longest x12 39.3 us: halve(): lax.ppermute(send.astype(jnp.bfloat16), axis, [(i, i ^ 1 << bit) for i in...]
    all_gather x2, waiting for transfers between devices: 0.02 us -> 37.8 us  [the longest x1 37.8 us: body(): first = lax.all_gather(conv_weight, ('ha', 'wa'), axis=0, tiled=True)]
    slice x14 -> x23, local copies, waits for them, and re-layouts: 17.1 us -> 42.5 us  [the longest x4 20.2 us: body(): turned[a]]
    reshape x12 -> x11, local copies, waits for them, and re-layouts: 41.7 us -> 16.5 us  [the longest x1 9.16 us: body(): first.reshape(3, 9, channels, channels)]
    another operation x0 -> x14, local copies, waits for them, and re-layouts: none -> 21.7 us  [the longest x8 12.1 us: flat_cells(): cells = window.reshape(frames, height * breadth, channels)]
  transfers between devices with their start and end apart: 18 -> 26, of which waited for: 2 -> 8; matrix products, arithmetic and copies ran while one was open for 33% -> 45% of each run, Pallas kernels for 0% -> 0%
where the time goes in v1:
time: 378 us; the launch traced here: 372 us
  local copies, waits for them, and re-layouts  127 us (34%)
  waiting for transfers between devices  81.8 us (22%)
  matrix products  50.2 us (13%)
  starting transfers between devices  50 us (13%)
  other arithmetic  48.5 us (13%)
  between operations  15.2 us (4%)
    ppermute x12, waiting for transfers between devices, halve(): lax.ppermute(send.astype(jnp.bfloat16), axis, [(i, i ^ 1 << bit) for i in...  39.3 us
    all_gather x1, waiting for transfers between devices, body(): first = lax.all_gather(conv_weight, ('ha', 'wa'), axis=0, tiled=True)  37.8 us
    unnamed x87, local copies, waits for them, and re-layouts  32.6 us
    ppermute x6, starting transfers between devices, with_halo(): lax.ppermute(lax.slice_in_dim(block, block.shape[dim] - 1, None, axis=dim...  22.5 us
    slice x4, local copies, waits for them, and re-layouts, body(): turned[a]  20.2 us
    ppermute x12, starting transfers between devices, halve(): lax.ppermute(send.astype(jnp.bfloat16), axis, [(i, i ^ 1 << bit) for i in...  19.1 us
    dot_general x3, matrix products, body(): jnp.dot(grad_taps[start:start + long], turned[a], preferred_element_type=...  14 us
    dot_general x3, matrix products, body(): lax.dot_general(taps[a * plane:a * plane + length], grad_hidden, over_row...  12.7 us
  transfers between devices with their start and end apart: 26, of which 8 were waited for; matrix products, arithmetic and copies ran while one was open for 45% of the time, Pallas kernels for 0%

profile of v1, /device:TPU:0, one launch (start us, length us, event | category | flops | bytes accessed | tf_op | source)
XLA Modules:
  0.0 372.5 jit_solution(198306464365348377)
XLA Ops:
  26.1 5.1 %collective-permute-start.4 = (bf16[5,1,40,384]{3,2,1,0:T(8,128)(2,1)S(1)}, bf16[5,1,40,384]{3,2,1,0:T(8,128)(2,1)S(1)}, u32[]{:S(2)}, u32[]{:S(2)}) collective-permute-start(bf16[5,1,40,384]{3,2,1,0:T(8,128)(2,1)S(1)} %get-tuple-element.48), channel_id=1, source_target_pairs={{0,4},{4,8},{8,12},{12,16},{16,20},{20,24},{24,28},{1,5},{5,9},{9,... | collective-permute-start | bytes 460808 | tf_op jit(solution)/shard_map/ppermute | solution.py:16
  36.4 4.3 %collective-permute-start.6 = (bf16[5,12,1,384]{3,2,1,0:T(2,128)(2,1)S(1)}, bf16[5,12,1,384]{3,2,1,0:T(2,128)(2,1)S(1)}, u32[]{:S(2)}, u32[]{:S(2)}) collective-permute-start(bf16[5,12,1,384]{3,2,1,0:T(2,128)(2,1)S(1)} %get-tuple-element.37), channel_id=1, source_target_pairs={{0,1},{1,2},{2,3},{4,5},{5,6},{6,7},{8,9},{9,10},{10,11},{12,13},{... | collective-permute-start | bytes 138248 | tf_op jit(solution)/shard_map/ppermute | solution.py:16
  86.7 4.6 %slice_convert_fusion = f32[32,108,384]{2,1,0:T(8,128)} fusion(bf16[32,112,384]{2,1,0:T(8,128)(2,1)} %bitcast.178), kind=kLoop, calls=%fused_computation.15 | loop fusion | flops 1327104 | bytes 7962624 | tf_op jit(solution)/shard_map/transpose | solution.py:89
  91.3 5.5 %reshape.304 = f32[3,3,384,384]{3,2,1,0:T(8,128)} reshape(f32[32,108,384]{2,1,0:T(8,128)} %slice_convert_fusion) | data formatting | bytes 10616832 | tf_op jit(solution)/shard_map/transpose | solution.py:89
  105.6 6.7 %copy.44 = bf16[4,4,384,384]{3,2,1,0:T(8,128)(2,1)} copy(bf16[4,4,384,384]{2,3,1,0:T(8,128)(2,1)} %pad_maximum_fusion.1) | data formatting | bytes 9437184 | tf_op jit(solution)/shard_map/stack | solution.py:94
  112.3 37.8 %all-gather.7.cloned.1.call-done = bf16[32,324,384]{2,1,0:T(8,128)(2,1)} async-done(((bf16[1,324,384]{2,1,0:T(8,128)(2,1)}), bf16[32,324,384]{2,1,0:T(8,128)(2,1)}) %all-gather.7.cloned.1.call-update) | async-done | bytes 7962640 | tf_op jit(solution)/shard_map/all_gather | solution.py:79
  150.1 9.3 %reshape.307 = bf16[10368,384]{1,0:T(8,128)(2,1)} reshape(bf16[32,324,384]{2,1,0:T(8,128)(2,1)} %all-gather.7.cloned.1.call-done) | data formatting | bytes 15925248
  159.4 5.3 %fusion.3 = f32[560,384]{1,0:T(8,128)S(1)} fusion(bf16[560,3456]{1,0:T(8,128)(2,1)} %bitcast.167, bf16[10368,384]{1,0:T(8,128)(2,1)} %reshape.307), kind=kOutput, calls=%fused_computation.17 | convolution fusion | flops 1486356480 | bytes 7385088 | tf_op jit(solution)/shard_map/dot_general | solution.py:105
  170.4 6.6 %fusion.46 = f32[384,6144]{1,0:T(8,128)S(1)} fusion(bf16[560,6144]{1,0:T(8,128)(2,1)} %bitcast.13, f32[560,384]{1,0:T(8,128)S(1)} %get-tuple-element.82, f32[384]{0:T(512)S(1)} %reshape.293, f32[560]{0:T(1024)S(1)} %add_rsqrt_fusion), kind=kOutput, calls=%fused_computation.162 | convolution fusion | flops 2643916800 | bytes 17182400 | tf_op jit(solution)/shard_map/dot_general | solution.py:137
  177.0 7.1 %multiply_reduce_fusion = (f32[384]{0:T(512)S(1)}, f32[560]{0:T(1024)S(1)}, f32[560,384]{1,0:T(8,128)S(1)}) fusion(f32[560,384]{1,0:T(8,128)S(1)} %get-tuple-element.82, f32[560]{0:T(1024)S(1)} %add_rsqrt_fusion, f32[384]{0:T(512)S(1)} %reshape.293, bf16[560,6144]{1,0:T(8,128)(2,1)} %bitcast.13, bf16[6144,384]{1,0:T(8,128)(2,1)S(1)} %bitcast.166), kind=kOutput, calls=%fused_computation.67 | convolution fusion | flops 2645851136 | bytes 13327744 | tf_op jit(solution)/shard_map/dot_general | solution.py:95
  192.7 4.4 %fusion.2 = bf16[3456,384]{1,0:T(8,128)(2,1)} fusion(bf16[560,3456]{1,0:T(8,128)(2,1)S(1)} %bitcast.168, bf16[560,384]{1,0:T(8,128)(2,1)S(1)} %multiply_convert_fusion.1), kind=kOutput, calls=%fused_computation.10 | convolution fusion | flops 1489010688 | bytes 6955008 | tf_op jit(solution)/shard_map/dot_general | solution.py:125
  204.0 9.3 %pad_maximum_fusion = bf16[10368,384]{1,0:T(8,128)(2,1)S(1)} fusion(bf16[3456,384]{1,0:T(8,128)(2,1)} %fusion.2, bf16[3456,384]{1,0:T(8,128)(2,1)} %fusion.1, bf16[3456,384]{1,0:T(8,128)(2,1)} %fusion), kind=kLoop, calls=%fused_computation.3 | loop fusion | flops 23887872 | bytes 15925248 | tf_op jit(solution)/shard_map/concatenate | solution.py:122
  220.3 9.2 %reshape.273 = bf16[3,9,384,384]{3,2,1,0:T(8,128)(2,1)} reshape(bf16[32,324,384]{2,1,0:T(8,128)(2,1)} %all-gather.7.cloned.1.call-done) | data formatting | bytes 15925248 | tf_op jit(solution)/shard_map/reshape | solution.py:193
  232.6 5.2 %collective-permute-start.11 = (bf16[5,7,1,384]{3,2,1,0:T(2,128)(2,1)}, bf16[5,7,1,384]{3,2,1,0:T(2,128)(2,1)}, u32[]{:S(2)}, u32[]{:S(2)}) collective-permute-start(bf16[5,7,1,384]{3,2,1,0:T(2,128)(2,1)} %get-tuple-element.69), channel_id=1, source_target_pairs={{0,1},{1,2},{2,3},{4,5},{5,6},{6,7},{8,9},{9,10},{10,11},{12,13},{... | collective-permute-start | bytes 80648 | tf_op jit(solution)/shard_map/ppermute | solution.py:16
  237.8 5.4 %fusion.88 = (bf16[1,9,384,384]{2,3,1,0:T(8,128)(2,1)S(1)}, bf16[1,9,384,384]{2,3,1,0:T(8,128)(2,1)}, bf16[1,9,384,384]{2,3,1,0:T(8,128)(2,1)}) fusion(bf16[3,9,384,384]{2,3,1,0:T(8,128)(2,1)} %bitcast.160), kind=kLoop, calls=%fused_computation.232 | loop fusion | bytes 15925248 | tf_op jit(solution)/shard_map/slice | solution.py:199
  243.2 5.3 %copy.46 = bf16[1,9,384,384]{3,2,1,0:T(8,128)(2,1)} copy(bf16[1,9,384,384]{2,3,1,0:T(8,128)(2,1)} %get-tuple-element.10) | data formatting | bytes 5308416 | tf_op jit(solution)/shard_map/slice | solution.py:199
  248.5 5.2 %copy.47 = bf16[1,9,384,384]{3,2,1,0:T(8,128)(2,1)} copy(bf16[1,9,384,384]{2,3,1,0:T(8,128)(2,1)} %get-tuple-element.9) | data formatting | bytes 5308416 | tf_op jit(solution)/shard_map/slice | solution.py:199
  253.7 4.3 %copy.48 = bf16[1,9,384,384]{3,2,1,0:T(8,128)(2,1)} copy(bf16[1,9,384,384]{2,3,1,0:T(8,128)(2,1)S(1)} %get-tuple-element.8) | data formatting | bytes 5308416 | tf_op jit(solution)/shard_map/slice | solution.py:199
  293.6 5.3 %collective-permute-done.20 = bf16[2,448,384]{2,1,0:T(8,128)(2,1)} collective-permute-done((bf16[2,448,384]{2,1,0:T(8,128)(2,1)}, bf16[2,448,384]{2,1,0:T(8,128)(2,1)}, u32[]{:S(2)}, u32[]{:S(2)}) %collective-permute-start.20) | collective-permute-done | bytes 688160 | tf_op jit(solution)/shard_map/ppermute | solution.py:48
  303.4 7.9 %collective-permute-done.15 = bf16[2,648,384]{2,1,0:T(8,128)(2,1)S(1)} collective-permute-done((bf16[2,648,384]{2,1,0:T(8,128)(2,1)S(1)}, bf16[2,648,384]{2,1,0:T(8,128)(2,1)S(1)}, u32[]{:S(2)}, u32[]{:S(2)}) %collective-permute-start.15) | collective-permute-done | bytes 995360 | tf_op jit(solution)/shard_map/ppermute | solution.py:48
  313.2 6.9 %collective-permute-done.13 = bf16[2,648,384]{2,1,0:T(8,128)(2,1)S(1)} collective-permute-done((bf16[2,648,384]{2,1,0:T(8,128)(2,1)S(1)}, bf16[2,648,384]{2,1,0:T(8,128)(2,1)S(1)}, u32[]{:S(2)}, u32[]{:S(2)}) %collective-permute-start.13) | collective-permute-done | bytes 995360 | tf_op jit(solution)/shard_map/ppermute | solution.py:48
  325.6 4.7 %collective-permute-done.16 = bf16[648,384]{1,0:T(8,128)(2,1)} collective-permute-done((bf16[648,384]{1,0:T(8,128)(2,1)}, bf16[648,384]{1,0:T(8,128)(2,1)}, u32[]{:S(2)}, u32[]{:S(2)}) %collective-permute-start.16) | collective-permute-done | bytes 497696 | tf_op jit(solution)/shard_map/ppermute | solution.py:48
  339.6 5.7 %fusion.11 = bf16[784,384]{1,0:T(8,128)(2,1)S(1)} fusion(f32[784,384]{1,0:T(8,128)S(1)} %copy-done.21, bf16[784,3456]{1,0:T(8,128)(2,1)} %bitcast.161, bf16[3456,384]{1,0:T(8,128)(2,1)S(1)} %bitcast.179), kind=kOutput, calls=%fused_computation.40 | convolution fusion | flops 2081501184 | bytes 9879552 | tf_op jit(solution)/shard_map/dot_general | solution.py:198
  354.3 10.3 %collective-permute-done.18 = bf16[324,384]{1,0:T(8,128)(2,1)S(1)} collective-permute-done((bf16[324,384]{1,0:T(8,128)(2,1)S(1)}, bf16[324,384]{1,0:T(8,128)(2,1)S(1)}, u32[]{:S(2)}, u32[]{:S(2)}) %collective-permute-start.18) | collective-permute-done | bytes 248864 | tf_op jit(solution)/shard_map/ppermute | solution.py:48
  (246 shorter events, 176.2 us)
Async XLA Ops:
  7.2 78.5 %all-gather.5.cloned.1.call-start = ((), (), s32[]{:S(2)}) async-start(), calls=%async_computation | async-start | bytes 2838528 | tf_op jit(solution)/shard_map/all_gather | solution.py:74
  8.8 141.4 %all-gather.7.cloned.1.call-start = ((), (), s32[]{:S(2)}) async-start(), calls=%async_computation.1 | async-start | bytes 8312832 | tf_op jit(solution)/shard_map/all_gather | solution.py:79
  12.9 5.3 %collective-permute-start.1 = (bf16[7,1,20,384]{3,0,2,1:T(8,128)(2,1)S(1)}, bf16[7,1,20,384]{3,0,2,1:T(8,128)(2,1)S(1)}, u32[]{:S(2)}, u32[]{:S(2)}) collective-permute-start(bf16[7,1,20,384]{3,0,2,1:T(8,128)(2,1)S(1)} %get-tuple-element.74), channel_id=1, source_target_pairs={{4,0},{8,4},{12,8},{16,12},{20,16},{24,20},{28,24},{5,1},{9,5},{13... | collective-permute-start | bytes 322568 | tf_op jit(solution)/shard_map/ppermute | solution.py:19
  20.3 12.3 %collective-permute-start.2 = (bf16[7,7,1,384]{3,0,2,1:T(8,128)(2,1)S(1)}, bf16[7,7,1,384]{3,0,2,1:T(8,128)(2,1)S(1)}, u32[]{:S(2)}, u32[]{:S(2)}) collective-permute-start(bf16[7,7,1,384]{3,0,2,1:T(8,128)(2,1)S(1)} %get-tuple-element.59), channel_id=1, source_target_pairs={{0,1},{1,2},{2,3},{4,5},{5,6},{6,7},{8,9},{9,10},{10,11},{12,13},{... | collective-permute-start | bytes 112904 | tf_op jit(solution)/shard_map/ppermute | solution.py:16
  23.8 8.8 %collective-permute-start.3 = (bf16[7,7,1,384]{3,0,2,1:T(8,128)(2,1)S(1)}, bf16[7,7,1,384]{3,0,2,1:T(8,128)(2,1)S(1)}, u32[]{:S(2)}, u32[]{:S(2)}) collective-permute-start(bf16[7,7,1,384]{3,0,2,1:T(8,128)(2,1)S(1)} %get-tuple-element.58), channel_id=1, source_target_pairs={{1,0},{2,1},{3,2},{5,4},{6,5},{7,6},{9,8},{10,9},{11,10},{13,12},{... | collective-permute-start | bytes 112904 | tf_op jit(solution)/shard_map/ppermute | solution.py:19
  26.1 9.6 %collective-permute-start.4 = (bf16[5,1,40,384]{3,2,1,0:T(8,128)(2,1)S(1)}, bf16[5,1,40,384]{3,2,1,0:T(8,128)(2,1)S(1)}, u32[]{:S(2)}, u32[]{:S(2)}) collective-permute-start(bf16[5,1,40,384]{3,2,1,0:T(8,128)(2,1)S(1)} %get-tuple-element.48), channel_id=1, source_target_pairs={{0,4},{4,8},{8,12},{12,16},{16,20},{20,24},{24,28},{1,5},{5,9},{9,... | collective-permute-start | bytes 460808 | tf_op jit(solution)/shard_map/ppermute | solution.py:16
  36.4 15.8 %collective-permute-start.6 = (bf16[5,12,1,384]{3,2,1,0:T(2,128)(2,1)S(1)}, bf16[5,12,1,384]{3,2,1,0:T(2,128)(2,1)S(1)}, u32[]{:S(2)}, u32[]{:S(2)}) collective-permute-start(bf16[5,12,1,384]{3,2,1,0:T(2,128)(2,1)S(1)} %get-tuple-element.37), channel_id=1, source_target_pairs={{0,1},{1,2},{2,3},{4,5},{5,6},{6,7},{8,9},{9,10},{10,11},{12,13},{... | collective-permute-start | bytes 138248 | tf_op jit(solution)/shard_map/ppermute | solution.py:16
  40.7 11.6 %collective-permute-start.7 = (bf16[5,12,1,384]{3,2,1,0:T(2,128)(2,1)S(1)}, bf16[5,12,1,384]{3,2,1,0:T(2,128)(2,1)S(1)}, u32[]{:S(2)}, u32[]{:S(2)}) collective-permute-start(bf16[5,12,1,384]{3,2,1,0:T(2,128)(2,1)S(1)} %get-tuple-element.38), channel_id=1, source_target_pairs={{1,0},{2,1},{3,2},{5,4},{6,5},{7,6},{9,8},{10,9},{11,10},{13,12},{... | collective-permute-start | bytes 138248 | tf_op jit(solution)/shard_map/ppermute | solution.py:19
  201.5 76.0 %collective-permute-start.19 = (bf16[2,2,448,384]{3,2,0,1:T(8,128)(2,1)}, bf16[2,2,448,384]{3,2,0,1:T(8,128)(2,1)}, u32[]{:S(2)}, u32[]{:S(2)}) collective-permute-start(bf16[2,2,448,384]{3,2,0,1:T(8,128)(2,1)} %bitcast.149), channel_id=1, source_target_pairs={{0,4},{4,0},{8,12},{12,8},{16,20},{20,16},{24,28},{28,24},{1,5},{5... | collective-permute-start | bytes 4128776 | tf_op jit(solution)/shard_map/ppermute | solution.py:48
  201.9 27.6 %collective-permute-start.8 = (bf16[5,1,20,384]{3,2,1,0:T(8,128)(2,1)S(1)}, bf16[5,1,20,384]{3,2,1,0:T(8,128)(2,1)S(1)}, u32[]{:S(2)}, u32[]{:S(2)}) collective-permute-start(bf16[5,1,20,384]{3,2,1,0:T(8,128)(2,1)S(1)} %get-tuple-element.80), channel_id=1, source_target_pairs={{0,4},{4,8},{8,12},{12,16},{16,20},{20,24},{24,28},{1,5},{5,9},{9,... | collective-permute-start | bytes 230408 | tf_op jit(solution)/shard_map/ppermute | solution.py:16
  217.8 64.6 %collective-permute-start.12 = (bf16[2,2,1296,384]{3,2,1,0:T(8,128)(2,1)}, bf16[2,2,1296,384]{3,2,1,0:T(8,128)(2,1)}, u32[]{:S(2)}, u32[]{:S(2)}) collective-permute-start(bf16[2,2,1296,384]{3,2,1,0:T(8,128)(2,1)} %dynamic-slice_bitcast_fusion), channel_id=1, source_target_pairs={{0,4},{4,0},{8,12},{12,8},{16,20},{20,16},{24,28},{28,24},{1,5},{5... | collective-permute-start | bytes 11943944 | tf_op jit(solution)/shard_map/ppermute | solution.py:48
  219.1 10.5 %collective-permute-start.9 = (bf16[5,1,20,384]{3,2,1,0:T(8,128)(2,1)S(1)}, bf16[5,1,20,384]{3,2,1,0:T(8,128)(2,1)S(1)}, u32[]{:S(2)}, u32[]{:S(2)}) collective-permute-start(bf16[5,1,20,384]{3,2,1,0:T(8,128)(2,1)S(1)} %get-tuple-element.79), channel_id=1, source_target_pairs={{4,0},{8,4},{12,8},{16,12},{20,16},{24,20},{28,24},{5,1},{9,5},{13... | collective-permute-start | bytes 230408 | tf_op jit(solution)/shard_map/ppermute | solution.py:19
  231.3 29.3 %collective-permute-start.10 = (bf16[5,7,1,384]{3,2,1,0:T(2,128)(2,1)}, bf16[5,7,1,384]{3,2,1,0:T(2,128)(2,1)}, u32[]{:S(2)}, u32[]{:S(2)}) collective-permute-start(bf16[5,7,1,384]{3,2,1,0:T(2,128)(2,1)} %get-tuple-element.70), channel_id=1, source_target_pairs={{1,0},{2,1},{3,2},{5,4},{6,5},{7,6},{9,8},{10,9},{11,10},{13,12},{... | collective-permute-start | bytes 80648 | tf_op jit(solution)/shard_map/ppermute | solution.py:19
  232.6 28.1 %collective-permute-start.11 = (bf16[5,7,1,384]{3,2,1,0:T(2,128)(2,1)}, bf16[5,7,1,384]{3,2,1,0:T(2,128)(2,1)}, u32[]{:S(2)}, u32[]{:S(2)}) collective-permute-start(bf16[5,7,1,384]{3,2,1,0:T(2,128)(2,1)} %get-tuple-element.69), channel_id=1, source_target_pairs={{0,1},{1,2},{2,3},{4,5},{5,6},{6,7},{8,9},{9,10},{10,11},{12,13},{... | collective-permute-start | bytes 80648 | tf_op jit(solution)/shard_map/ppermute | solution.py:16
  280.1 18.8 %collective-permute-start.20 = (bf16[2,448,384]{2,1,0:T(8,128)(2,1)}, bf16[2,448,384]{2,1,0:T(8,128)(2,1)}, u32[]{:S(2)}, u32[]{:S(2)}) collective-permute-start(bf16[2,448,384]{2,1,0:T(8,128)(2,1)} %fusion.21), channel_id=1, source_target_pairs={{0,8},{4,12},{8,0},{12,4},{16,24},{20,28},{24,16},{28,20},{1,9},{5... | collective-permute-start | bytes 2064392 | tf_op jit(solution)/shard_map/ppermute | solution.py:48
  286.2 25.0 %collective-permute-start.15 = (bf16[2,648,384]{2,1,0:T(8,128)(2,1)S(1)}, bf16[2,648,384]{2,1,0:T(8,128)(2,1)S(1)}, u32[]{:S(2)}, u32[]{:S(2)}) collective-permute-start(bf16[2,648,384]{2,1,0:T(8,128)(2,1)S(1)} %fusion.20), channel_id=1, source_target_pairs={{0,16},{4,20},{8,24},{12,28},{16,0},{20,4},{24,8},{28,12},{1,17},{... | collective-permute-start | bytes 2985992 | tf_op jit(solution)/shard_map/ppermute | solution.py:48
  287.3 32.8 %collective-permute-start.13 = (bf16[2,648,384]{2,1,0:T(8,128)(2,1)S(1)}, bf16[2,648,384]{2,1,0:T(8,128)(2,1)S(1)}, u32[]{:S(2)}, u32[]{:S(2)}) collective-permute-start(bf16[2,648,384]{2,1,0:T(8,128)(2,1)S(1)} %fusion.19), channel_id=1, source_target_pairs={{0,8},{4,12},{8,0},{12,4},{16,24},{20,28},{24,16},{28,20},{1,9},{5... | collective-permute-start | bytes 2985992 | tf_op jit(solution)/shard_map/ppermute | solution.py:48
  300.2 24.1 %collective-permute-start.21 = (bf16[448,384]{1,0:T(8,128)(2,1)S(1)}, bf16[448,384]{1,0:T(8,128)(2,1)S(1)}, u32[]{:S(2)}, u32[]{:S(2)}) collective-permute-start(bf16[448,384]{1,0:T(8,128)(2,1)S(1)} %fusion.55), channel_id=1, source_target_pairs={{0,16},{4,20},{8,24},{12,28},{16,0},{20,4},{24,8},{28,12},{1,17},{... | collective-permute-start | bytes 1032200 | tf_op jit(solution)/shard_map/ppermute | solution.py:48
  312.3 18.0 %collective-permute-start.16 = (bf16[648,384]{1,0:T(8,128)(2,1)}, bf16[648,384]{1,0:T(8,128)(2,1)}, u32[]{:S(2)}, u32[]{:S(2)}) collective-permute-start(bf16[648,384]{1,0:T(8,128)(2,1)} %fusion.41), channel_id=1, source_target_pairs={{0,8},{4,12},{8,0},{12,4},{16,24},{20,28},{24,16},{28,20},{1,9},{5... | collective-permute-start | bytes 1493000 | tf_op jit(solution)/shard_map/ppermute | solution.py:48
  321.3 12.5 %collective-permute-start.14 = (bf16[648,384]{1,0:T(8,128)(2,1)}, bf16[648,384]{1,0:T(8,128)(2,1)}, u32[]{:S(2)}, u32[]{:S(2)}) collective-permute-start(bf16[648,384]{1,0:T(8,128)(2,1)} %fusion.40), channel_id=1, source_target_pairs={{0,16},{4,20},{8,24},{12,28},{16,0},{20,4},{24,8},{28,12},{1,17},{... | collective-permute-start | bytes 1493000 | tf_op jit(solution)/shard_map/ppermute | solution.py:48
  324.6 21.6 %collective-permute-start.22 = (bf16[2,109,384]{2,1,0:T(8,128)(2,1)S(1)}, bf16[2,109,384]{2,1,0:T(8,128)(2,1)S(1)}, u32[]{:S(2)}, u32[]{:S(2)}) collective-permute-start(bf16[2,109,384]{2,1,0:T(8,128)(2,1)S(1)} %fusion.82), channel_id=1, source_target_pairs={{0,1},{1,0},{2,3},{3,2},{4,5},{5,4},{6,7},{7,6},{8,9},{9,8},{10,11... | collective-permute-start | bytes 502280 | tf_op jit(solution)/shard_map/ppermute | solution.py:48
  337.7 14.6 %collective-permute-start.17 = (bf16[2,324,384]{2,1,0:T(8,128)(2,1)S(1)}, bf16[2,324,384]{2,1,0:T(8,128)(2,1)S(1)}, u32[]{:S(2)}, u32[]{:S(2)}) collective-permute-start(bf16[2,324,384]{2,1,0:T(8,128)(2,1)S(1)} %fusion.39), channel_id=1, source_target_pairs={{0,1},{1,0},{2,3},{3,2},{4,5},{5,4},{6,7},{7,6},{8,9},{9,8},{10,11... | collective-permute-start | bytes 1493000 | tf_op jit(solution)/shard_map/ppermute | solution.py:48
  346.3 7.5 %collective-permute-start.23 = (bf16[109,384]{1,0:T(8,128)(2,1)S(1)}, bf16[109,384]{1,0:T(8,128)(2,1)S(1)}, u32[]{:S(2)}, u32[]{:S(2)}) collective-permute-start(bf16[109,384]{1,0:T(8,128)(2,1)S(1)} %fusion.85), channel_id=1, source_target_pairs={{0,2},{1,3},{2,0},{3,1},{4,6},{5,7},{6,4},{7,5},{8,10},{9,11},{10,... | collective-permute-start | bytes 251144 | tf_op jit(solution)/shard_map/ppermute | solution.py:48
  352.5 12.1 %collective-permute-start.18 = (bf16[324,384]{1,0:T(8,128)(2,1)S(1)}, bf16[324,384]{1,0:T(8,128)(2,1)S(1)}, u32[]{:S(2)}, u32[]{:S(2)}) collective-permute-start(bf16[324,384]{1,0:T(8,128)(2,1)S(1)} %fusion.81), channel_id=1, source_target_pairs={{0,2},{1,3},{2,0},{3,1},{4,6},{5,7},{6,4},{7,5},{8,10},{9,11},{10,... | collective-permute-start | bytes 746504 | tf_op jit(solution)/shard_map/ppermute | solution.py:48
  (31 other events, 158.2 us)
Sparse Core Ops, SparseCore 0:
  11.4 60.9 all-gather.4
  75.2 74.9 all-gather.6

commit v2 on v1

--- a/solution.py
+++ b/solution.py
@@ -163,7 +163,14 @@
     )
     small = jnp.concatenate([local_second.reshape(n_ha, up_part, channels), gain_part], axis=1)
     small = small.reshape((2,) * len(ha_bits) + small.shape[1:])
-    small = halve(small, "ha", ha_bits, ha_bits[::-1])
+    small = halve(small, "ha", [0], ha_bits[::-1])
+
+    part = local_first.shape[0] // n_ha
+    big = local_first.reshape((2,) * len(ha_bits) + (part, channels))
+    big = halve(big, "ha", [0], ha_bits[::-1])
+    left = ha_bits[:0:-1]
+    first, big, small = lax.optimization_barrier((first, big, small))
+    small = halve(small, "ha", ha_bits[1:], left)
     ups = small[:up_part].reshape(n_wa, up_rows, channels)
     small = jnp.concatenate([ups, small[up_part : up_part + n_wa][:, None]], axis=1)
     small = small.reshape((2,) * len(wa_bits) + small.shape[1:])
@@ -171,10 +178,6 @@
     upconv_grad = small[:up_rows]
     gain_grad = small[up_rows, :own_gain]
 
-    part = local_first.shape[0] // n_ha
-    big = local_first.reshape((2,) * len(ha_bits) + (part, channels))
-    big = halve(big, "ha", [0], ha_bits[::-1])
-    left = ha_bits[:0:-1]
     ends = []
     for side, order in ((0, ha_bits[1:]), (1, left)):
         half = big[..., side * part // 2 : (side + 1) * part // 2, :]

time: 378 us -> 410 us (1.085)
  other arithmetic: 48.5 us -> 73.6 us
  matrix products: 50.2 us -> 54.4 us
    slice x4 -> x1, local copies, waits for them, and re-layouts: 20.2 us -> 5.45 us  [body(): turned[a]]
    concatenate x1, other arithmetic: 9.3 us -> 23.9 us  [body(): jnp.concatenate([(lax.dot_general(taps[a * plane:a * plane + length], gra...]
    optimization_barrier x0 -> x1, local copies, waits for them, and re-layouts: none -> 9.31 us  [body(): first, big, small = lax.optimization_barrier((first, big, small))]
    unnamed x12 -> x14, other arithmetic: 1.6 us -> 8.52 us
    unnamed x87 -> x108, local copies, waits for them, and re-layouts: 32.6 us -> 26.2 us
    ppermute x12, waiting for transfers between devices: 39.3 us -> 44.2 us  [halve(): lax.ppermute(send.astype(jnp.bfloat16), axis, [(i, i ^ 1 << bit) for i in...]
  transfers between devices with their start and end apart: 26 -> 26, of which waited for: 8 -> 8; matrix products, arithmetic and copies ran while one was open for 45% -> 42% of each run, Pallas kernels for 0% -> 0%
where the time goes in v2:
time: 410 us; the launch traced here: 405 us
  local copies, waits for them, and re-layouts  128 us (31%)
  waiting for transfers between devices  85 us (21%)
  other arithmetic  73.6 us (18%)
  matrix products  54.4 us (13%)
  starting transfers between devices  48.6 us (12%)
  between operations  15.3 us (4%)
    ppermute x12, waiting for transfers between devices, halve(): lax.ppermute(send.astype(jnp.bfloat16), axis, [(i, i ^ 1 << bit) for i in...  44.2 us
    all_gather x1, waiting for transfers between devices, body(): first = lax.all_gather(conv_weight, ('ha', 'wa'), axis=0, tiled=True)  36.1 us
    unnamed x108, local copies, waits for them, and re-layouts  26.2 us
    concatenate x1, other arithmetic, body(): jnp.concatenate([(lax.dot_general(taps[a * plane:a * plane + length], gra...  23.9 us
    ppermute x6, starting transfers between devices, with_halo(): lax.ppermute(lax.slice_in_dim(block, block.shape[dim] - 1, None, axis=dim...  23.5 us
    ppermute x12, starting transfers between devices, halve(): lax.ppermute(send.astype(jnp.bfloat16), axis, [(i, i ^ 1 << bit) for i in...  16.3 us
    dot_general x3, matrix products, body(): jnp.dot(grad_taps[start:start + long], turned[a], preferred_element_type=...  15.2 us
    add x12, other arithmetic, halve(): block = keep.astype(jnp.float32) + got.astype(jnp.float32)  14.2 us
  transfers between devices with their start and end apart: 26, of which 8 were waited for; matrix products, arithmetic and copies ran while one was open for 42% of the time, Pallas kernels for 0%

profile of v2, /device:TPU:0, one launch (start us, length us, event | category | flops | bytes accessed | tf_op | source)
XLA Modules:
  0.0 404.6 jit_solution(18375126541901495759)
XLA Ops:
  21.4 4.5 %collective-permute-start.2 = (bf16[7,7,1,384]{3,0,2,1:T(8,128)(2,1)S(1)}, bf16[7,7,1,384]{3,0,2,1:T(8,128)(2,1)S(1)}, u32[]{:S(2)}, u32[]{:S(2)}) collective-permute-start(bf16[7,7,1,384]{3,0,2,1:T(8,128)(2,1)S(1)} %get-tuple-element.65), channel_id=1, source_target_pairs={{0,1},{1,2},{2,3},{4,5},{5,6},{6,7},{8,9},{9,10},{10,11},{12,13},{... | collective-permute-start | bytes 112904 | tf_op jit(solution)/shard_map/ppermute | solution.py:16
  28.3 5.5 %collective-permute-start.4 = (bf16[5,1,40,384]{3,2,1,0:T(8,128)(2,1)S(1)}, bf16[5,1,40,384]{3,2,1,0:T(8,128)(2,1)S(1)}, u32[]{:S(2)}, u32[]{:S(2)}) collective-permute-start(bf16[5,1,40,384]{3,2,1,0:T(8,128)(2,1)S(1)} %get-tuple-element.54), channel_id=1, source_target_pairs={{0,4},{4,8},{8,12},{12,16},{16,20},{20,24},{24,28},{1,5},{5,9},{9,... | collective-permute-start | bytes 460808 | tf_op jit(solution)/shard_map/ppermute | solution.py:16
  88.6 4.6 %slice_convert_fusion = f32[32,108,384]{2,1,0:T(8,128)} fusion(bf16[32,112,384]{2,1,0:T(8,128)(2,1)} %bitcast.184), kind=kLoop, calls=%fused_computation.15 | loop fusion | flops 1327104 | bytes 7962624 | tf_op jit(solution)/shard_map/transpose | solution.py:89
  93.2 5.6 %reshape.304 = f32[3,3,384,384]{3,2,1,0:T(8,128)} reshape(f32[32,108,384]{2,1,0:T(8,128)} %slice_convert_fusion) | data formatting | bytes 10616832 | tf_op jit(solution)/shard_map/transpose | solution.py:89
  107.4 6.7 %copy.40 = bf16[4,4,384,384]{3,2,1,0:T(8,128)(2,1)} copy(bf16[4,4,384,384]{2,3,1,0:T(8,128)(2,1)} %pad_maximum_fusion.1) | data formatting | bytes 9437184 | tf_op jit(solution)/shard_map/stack | solution.py:94
  114.0 36.1 %all-gather.7.cloned.1.call-done = bf16[32,324,384]{2,1,0:T(8,128)(2,1)} async-done(((bf16[1,324,384]{2,1,0:T(8,128)(2,1)}), bf16[32,324,384]{2,1,0:T(8,128)(2,1)}) %all-gather.7.cloned.1.call-update) | async-done | bytes 7962640 | tf_op jit(solution)/shard_map/all_gather | solution.py:79
  150.1 9.3 %reshape.307 = bf16[10368,384]{1,0:T(8,128)(2,1)} reshape(bf16[32,324,384]{2,1,0:T(8,128)(2,1)} %all-gather.7.cloned.1.call-done) | data formatting | bytes 15925248 | tf_op jit(solution)/shard_map/optimization_barrier | solution.py:172
  159.5 5.3 %fusion.3 = f32[560,384]{1,0:T(8,128)S(1)} fusion(bf16[560,3456]{1,0:T(8,128)(2,1)} %bitcast.175, bf16[10368,384]{1,0:T(8,128)(2,1)} %reshape.307), kind=kOutput, calls=%fused_computation.17 | convolution fusion | flops 1486356480 | bytes 7385088 | tf_op jit(solution)/shard_map/dot_general | solution.py:105
  170.5 7.2 %multiply_reduce_fusion = (f32[384]{0:T(512)S(1)}, f32[560]{0:T(1024)S(1)}, f32[560,384]{1,0:T(8,128)S(1)}) fusion(f32[560,384]{1,0:T(8,128)S(1)} %get-tuple-element.88, f32[560]{0:T(1024)S(1)} %add_rsqrt_fusion, f32[384]{0:T(512)S(1)} %reshape.293, bf16[560,6144]{1,0:T(8,128)(2,1)} %bitcast.13, bf16[6144,384]{1,0:T(8,128)(2,1)S(1)} %bitcast.172), kind=kOutput, calls=%fused_computation.67 | convolution fusion | flops 2645851136 | bytes 13327744 | tf_op jit(solution)/shard_map/dot_general | solution.py:95
  178.0 4.2 %fusion.2 = bf16[3456,384]{1,0:T(8,128)(2,1)} fusion(bf16[560,3456]{1,0:T(8,128)(2,1)S(1)} %bitcast.176, bf16[560,384]{1,0:T(8,128)(2,1)S(1)} %multiply_convert_fusion.1), kind=kOutput, calls=%fused_computation.10 | convolution fusion | flops 1489010688 | bytes 6955008 | tf_op jit(solution)/shard_map/dot_general | solution.py:125
  182.1 4.1 %fusion.1 = bf16[3456,384]{1,0:T(8,128)(2,1)} fusion(bf16[560,3456]{1,0:T(8,128)(2,1)S(1)} %bitcast.178, bf16[560,384]{1,0:T(8,128)(2,1)S(1)} %multiply_convert_fusion.1), kind=kOutput, calls=%fused_computation.9 | convolution fusion | flops 1489010688 | bytes 6955008 | tf_op jit(solution)/shard_map/dot_general | solution.py:125
  186.3 4.2 %fusion = bf16[3456,384]{1,0:T(8,128)(2,1)} fusion(bf16[560,3456]{1,0:T(8,128)(2,1)S(1)} %bitcast.174, bf16[560,384]{1,0:T(8,128)(2,1)S(1)} %multiply_convert_fusion.1), kind=kOutput, calls=%fused_computation.8 | convolution fusion | flops 1489010688 | bytes 6955008 | tf_op jit(solution)/shard_map/dot_general | solution.py:125
  190.4 9.6 %fusion.46 = f32[384,6144]{1,0:T(8,128)} fusion(bf16[560,6144]{1,0:T(8,128)(2,1)} %bitcast.13, f32[560,384]{1,0:T(8,128)S(1)} %get-tuple-element.88, f32[384]{0:T(512)S(1)} %reshape.293, f32[560]{0:T(1024)S(1)} %add_rsqrt_fusion), kind=kOutput, calls=%fused_computation.162 | convolution fusion | flops 2643916800 | bytes 17182400 | tf_op jit(solution)/shard_map/dot_general | solution.py:137
  216.8 23.9 %pad_maximum_fusion = bf16[10368,384]{1,0:T(8,128)(2,1)S(1)} fusion(bf16[3456,384]{1,0:T(8,128)(2,1)S(1)} %copy-done.17, bf16[3456,384]{1,0:T(8,128)(2,1)S(1)} %copy-done.18, bf16[3456,384]{1,0:T(8,128)(2,1)S(1)} %copy-done.19), kind=kLoop, calls=%fused_computation.3 | loop fusion | flops 23887872 | bytes 15925248 | tf_op jit(solution)/shard_map/concatenate | solution.py:122
  272.7 8.1 %pad_slice_fusion = (bf16[7,112,3456]{2,1,0:T(8,128)(2,1)}, bf16[7,112,3456]{2,1,0:T(8,128)(2,1)}, bf16[7,112,3456]{2,1,0:T(8,128)(2,1)}) fusion(bf16[5,112,3456]{2,1,0:T(8,128)(2,1)S(1)} %pad_dynamic-update-slice_fusion.17), kind=kLoop, calls=%fused_computation | loop fusion | bytes 20127744 | tf_op jit(solution)/shard_map/slice | solution.py:202
  282.5 6.3 %convert_add_fusion = f32[2,2,1296,384]{3,2,1,0:T(8,128)} fusion(bf16[2,2,1296,384]{3,2,1,0:T(8,128)(2,1)} %collective-permute-done.12, bf16[2,2,2,1296,384]{4,3,2,1,0:T(8,128)(2,1)S(1)} %bitcast.161, s32[]{:T(128)S(6)} %select_n.55), kind=kLoop, calls=%fused_computation.4 | loop fusion | flops 5971968 | bytes 15925252 | tf_op jit(solution)/shard_map/add | solution.py:51
  288.8 12.9 %copy.45 = bf16[3,9,384,384]{2,3,1,0:T(8,128)(2,1)} copy(bf16[3,9,384,384]{3,2,1,0:T(8,128)(2,1)} %bitcast.157) | data formatting | bytes 15925248 | tf_op jit(solution)/shard_map/reshape | solution.py:196
  301.7 5.5 %fusion.88 = (bf16[1,9,384,384]{3,2,1,0:T(8,128)(2,1)}, bf16[1,9,384,384]{3,2,1,0:T(8,128)(2,1)S(1)}, bf16[1,9,384,384]{3,2,1,0:T(8,128)(2,1)}) fusion(bf16[3,9,384,384]{3,2,1,0:T(8,128)(2,1)} %bitcast.164), kind=kLoop, calls=%fused_computation.232 | loop fusion | bytes 15925248 | tf_op jit(solution)/shard_map/slice | solution.py:202
  312.8 5.4 %fusion.97 = f32[784,384]{1,0:T(8,128)S(1)} fusion(bf16[784,3456]{1,0:T(8,128)(2,1)} %bitcast.169, bf16[3456,384]{1,0:T(8,128)(2,1)S(1)} %bitcast.187), kind=kOutput, calls=%fused_computation.241 | convolution fusion | flops 2080899072 | bytes 9277440 | tf_op jit(solution)/shard_map/dot_general | solution.py:201
  322.4 4.4 %collective-permute-done.20 = bf16[2,448,384]{2,1,0:T(8,128)(2,1)S(1)} collective-permute-done((bf16[2,448,384]{2,1,0:T(8,128)(2,1)}, bf16[2,448,384]{2,1,0:T(8,128)(2,1)S(1)}, u32[]{:S(2)}, u32[]{:S(2)}) %collective-permute-start.20) | collective-permute-done | bytes 688160 | tf_op jit(solution)/shard_map/ppermute | solution.py:48
  328.3 19.5 %collective-permute-done.14 = bf16[2,648,384]{2,1,0:T(8,128)(2,1)S(1)} collective-permute-done((bf16[2,648,384]{2,1,0:T(8,128)(2,1)S(1)}, bf16[2,648,384]{2,1,0:T(8,128)(2,1)S(1)}, u32[]{:S(2)}, u32[]{:S(2)}) %collective-permute-start.14) | collective-permute-done | bytes 995360 | tf_op jit(solution)/shard_map/ppermute | solution.py:48
  355.9 6.3 %collective-permute-done.15 = bf16[648,384]{1,0:T(8,128)(2,1)} collective-permute-done((bf16[648,384]{1,0:T(8,128)(2,1)}, bf16[648,384]{1,0:T(8,128)(2,1)}, u32[]{:S(2)}, u32[]{:S(2)}) %collective-permute-start.15) | collective-permute-done | bytes 497696 | tf_op jit(solution)/shard_map/ppermute | solution.py:48
  372.4 5.6 %fusion.11 = bf16[784,384]{1,0:T(8,128)(2,1)S(1)} fusion(f32[784,384]{1,0:T(8,128)S(1)} %copy-done.29, bf16[784,3456]{1,0:T(8,128)(2,1)} %bitcast.165, bf16[3456,384]{1,0:T(8,128)(2,1)S(1)} %bitcast.185), kind=kOutput, calls=%fused_computation.40 | convolution fusion | flops 2081501184 | bytes 9879552 | tf_op jit(solution)/shard_map/dot_general | solution.py:201
  389.4 7.3 %collective-permute-done.19 = bf16[324,384]{1,0:T(8,128)(2,1)S(1)} collective-permute-done((bf16[324,384]{1,0:T(8,128)(2,1)S(1)}, bf16[324,384]{1,0:T(8,128)(2,1)S(1)}, u32[]{:S(2)}, u32[]{:S(2)}) %collective-permute-start.19) | collective-permute-done | bytes 248864 | tf_op jit(solution)/shard_map/ppermute | solution.py:48
  (267 shorter events, 177.1 us)
Async XLA Ops:
  7.2 80.4 %all-gather.5.cloned.1.call-start = ((), (), s32[]{:S(2)}) async-start(), calls=%async_computation | async-start | bytes 2838528 | tf_op jit(solution)/shard_map/all_gather | solution.py:74
  8.8 141.3 %all-gather.7.cloned.1.call-start = ((), (), s32[]{:S(2)}) async-start(), calls=%async_computation.1 | async-start | bytes 8312832 | tf_op jit(solution)/shard_map/all_gather | solution.py:79
  20.1 13.7 %collective-permute-start.3 = (bf16[7,7,1,384]{3,0,2,1:T(8,128)(2,1)S(1)}, bf16[7,7,1,384]{3,0,2,1:T(8,128)(2,1)S(1)}, u32[]{:S(2)}, u32[]{:S(2)}) collective-permute-start(bf16[7,7,1,384]{3,0,2,1:T(8,128)(2,1)S(1)} %get-tuple-element.64), channel_id=1, source_target_pairs={{1,0},{2,1},{3,2},{5,4},{6,5},{7,6},{9,8},{10,9},{11,10},{13,12},{... | collective-permute-start | bytes 112904 | tf_op jit(solution)/shard_map/ppermute | solution.py:19
  21.4 12.4 %collective-permute-start.2 = (bf16[7,7,1,384]{3,0,2,1:T(8,128)(2,1)S(1)}, bf16[7,7,1,384]{3,0,2,1:T(8,128)(2,1)S(1)}, u32[]{:S(2)}, u32[]{:S(2)}) collective-permute-start(bf16[7,7,1,384]{3,0,2,1:T(8,128)(2,1)S(1)} %get-tuple-element.65), channel_id=1, source_target_pairs={{0,1},{1,2},{2,3},{4,5},{5,6},{6,7},{8,9},{9,10},{10,11},{12,13},{... | collective-permute-start | bytes 112904 | tf_op jit(solution)/shard_map/ppermute | solution.py:16
  27.0 10.5 %collective-permute-start.5 = (bf16[5,1,40,384]{3,2,1,0:T(8,128)(2,1)S(1)}, bf16[5,1,40,384]{3,2,1,0:T(8,128)(2,1)S(1)}, u32[]{:S(2)}, u32[]{:S(2)}) collective-permute-start(bf16[5,1,40,384]{3,2,1,0:T(8,128)(2,1)S(1)} %get-tuple-element.53), channel_id=1, source_target_pairs={{4,0},{8,4},{12,8},{16,12},{20,16},{24,20},{28,24},{5,1},{9,5},{13... | collective-permute-start | bytes 460808 | tf_op jit(solution)/shard_map/ppermute | solution.py:19
  28.3 8.6 %collective-permute-start.4 = (bf16[5,1,40,384]{3,2,1,0:T(8,128)(2,1)S(1)}, bf16[5,1,40,384]{3,2,1,0:T(8,128)(2,1)S(1)}, u32[]{:S(2)}, u32[]{:S(2)}) collective-permute-start(bf16[5,1,40,384]{3,2,1,0:T(8,128)(2,1)S(1)} %get-tuple-element.54), channel_id=1, source_target_pairs={{0,4},{4,8},{8,12},{12,16},{16,20},{20,24},{24,28},{1,5},{5,9},{9,... | collective-permute-start | bytes 460808 | tf_op jit(solution)/shard_map/ppermute | solution.py:16
  37.7 15.2 %collective-permute-start.6 = (bf16[5,12,1,384]{3,2,1,0:T(2,128)(2,1)S(1)}, bf16[5,12,1,384]{3,2,1,0:T(2,128)(2,1)S(1)}, u32[]{:S(2)}, u32[]{:S(2)}) collective-permute-start(bf16[5,12,1,384]{3,2,1,0:T(2,128)(2,1)S(1)} %get-tuple-element.43), channel_id=1, source_target_pairs={{0,1},{1,2},{2,3},{4,5},{5,6},{6,7},{8,9},{9,10},{10,11},{12,13},{... | collective-permute-start | bytes 138248 | tf_op jit(solution)/shard_map/ppermute | solution.py:16
  41.2 11.7 %collective-permute-start.7 = (bf16[5,12,1,384]{3,2,1,0:T(2,128)(2,1)S(1)}, bf16[5,12,1,384]{3,2,1,0:T(2,128)(2,1)S(1)}, u32[]{:S(2)}, u32[]{:S(2)}) collective-permute-start(bf16[5,12,1,384]{3,2,1,0:T(2,128)(2,1)S(1)} %get-tuple-element.44), channel_id=1, source_target_pairs={{1,0},{2,1},{3,2},{5,4},{6,5},{7,6},{9,8},{10,9},{11,10},{13,12},{... | collective-permute-start | bytes 138248 | tf_op jit(solution)/shard_map/ppermute | solution.py:19
  200.9 47.9 %collective-permute-start.9 = (bf16[5,1,20,384]{3,2,1,0:T(8,128)(2,1)}, bf16[5,1,20,384]{3,2,1,0:T(8,128)(2,1)}, u32[]{:S(2)}, u32[]{:S(2)}) collective-permute-start(bf16[5,1,20,384]{3,2,1,0:T(8,128)(2,1)} %get-tuple-element.85), channel_id=1, source_target_pairs={{4,0},{8,4},{12,8},{16,12},{20,16},{24,20},{28,24},{5,1},{9,5},{13... | collective-permute-start | bytes 230408 | tf_op jit(solution)/shard_map/ppermute | solution.py:19
  202.1 45.7 %collective-permute-start.8 = (bf16[5,1,20,384]{3,2,1,0:T(8,128)(2,1)}, bf16[5,1,20,384]{3,2,1,0:T(8,128)(2,1)}, u32[]{:S(2)}, u32[]{:S(2)}) collective-permute-start(bf16[5,1,20,384]{3,2,1,0:T(8,128)(2,1)} %get-tuple-element.86), channel_id=1, source_target_pairs={{0,4},{4,8},{8,12},{12,16},{16,20},{20,24},{24,28},{1,5},{5,9},{9,... | collective-permute-start | bytes 230408 | tf_op jit(solution)/shard_map/ppermute | solution.py:16
  245.2 37.2 %collective-permute-start.12 = (bf16[2,2,1296,384]{3,2,1,0:T(8,128)(2,1)}, bf16[2,2,1296,384]{3,2,1,0:T(8,128)(2,1)}, u32[]{:S(2)}, u32[]{:S(2)}) collective-permute-start(bf16[2,2,1296,384]{3,2,1,0:T(8,128)(2,1)} %dynamic-slice_bitcast_fusion), channel_id=1, source_target_pairs={{0,4},{4,0},{8,12},{12,8},{16,20},{20,16},{24,28},{28,24},{1,5},{5... | collective-permute-start | bytes 11943944 | tf_op jit(solution)/shard_map/ppermute | solution.py:48
  252.5 11.0 %collective-permute-start.11 = (bf16[5,7,1,384]{3,2,1,0:T(2,128)(2,1)}, bf16[5,7,1,384]{3,2,1,0:T(2,128)(2,1)}, u32[]{:S(2)}, u32[]{:S(2)}) collective-permute-start(bf16[5,7,1,384]{3,2,1,0:T(2,128)(2,1)} %get-tuple-element.75), channel_id=1, source_target_pairs={{0,1},{1,2},{2,3},{4,5},{5,6},{6,7},{8,9},{9,10},{10,11},{12,13},{... | collective-permute-start | bytes 80648 | tf_op jit(solution)/shard_map/ppermute | solution.py:16
  256.5 7.0 %collective-permute-start.10 = (bf16[5,7,1,384]{3,2,1,0:T(2,128)(2,1)}, bf16[5,7,1,384]{3,2,1,0:T(2,128)(2,1)}, u32[]{:S(2)}, u32[]{:S(2)}) collective-permute-start(bf16[5,7,1,384]{3,2,1,0:T(2,128)(2,1)} %get-tuple-element.76), channel_id=1, source_target_pairs={{1,0},{2,1},{3,2},{5,4},{6,5},{7,6},{9,8},{10,9},{11,10},{13,12},{... | collective-permute-start | bytes 80648 | tf_op jit(solution)/shard_map/ppermute | solution.py:19
  260.9 19.9 %collective-permute-start.13 = (bf16[2,2,448,384]{3,2,0,1:T(8,128)(2,1)}, bf16[2,2,448,384]{3,2,0,1:T(8,128)(2,1)}, u32[]{:S(2)}, u32[]{:S(2)}) collective-permute-start(bf16[2,2,448,384]{3,2,0,1:T(8,128)(2,1)} %bitcast.150), channel_id=1, source_target_pairs={{0,4},{4,0},{8,12},{12,8},{16,20},{20,16},{24,28},{28,24},{1,5},{5... | collective-permute-start | bytes 4128776 | tf_op jit(solution)/shard_map/ppermute | solution.py:48
  308.1 18.7 %collective-permute-start.20 = (bf16[2,448,384]{2,1,0:T(8,128)(2,1)}, bf16[2,448,384]{2,1,0:T(8,128)(2,1)S(1)}, u32[]{:S(2)}, u32[]{:S(2)}) collective-permute-start(bf16[2,448,384]{2,1,0:T(8,128)(2,1)} %fusion.21), channel_id=1, source_target_pairs={{0,8},{4,12},{8,0},{12,4},{16,24},{20,28},{24,16},{28,20},{1,9},{5... | collective-permute-start | bytes 2064392 | tf_op jit(solution)/shard_map/ppermute | solution.py:48
  311.1 36.7 %collective-permute-start.14 = (bf16[2,648,384]{2,1,0:T(8,128)(2,1)S(1)}, bf16[2,648,384]{2,1,0:T(8,128)(2,1)S(1)}, u32[]{:S(2)}, u32[]{:S(2)}) collective-permute-start(bf16[2,648,384]{2,1,0:T(8,128)(2,1)S(1)} %fusion.19), channel_id=1, source_target_pairs={{0,8},{4,12},{8,0},{12,4},{16,24},{20,28},{24,16},{28,20},{1,9},{5... | collective-permute-start | bytes 2985992 | tf_op jit(solution)/shard_map/ppermute | solution.py:48
  312.7 37.0 %collective-permute-start.16 = (bf16[2,648,384]{2,1,0:T(8,128)(2,1)S(1)}, bf16[2,648,384]{2,1,0:T(8,128)(2,1)S(1)}, u32[]{:S(2)}, u32[]{:S(2)}) collective-permute-start(bf16[2,648,384]{2,1,0:T(8,128)(2,1)S(1)} %fusion.20), channel_id=1, source_target_pairs={{0,16},{4,20},{8,24},{12,28},{16,0},{20,4},{24,8},{28,12},{1,17},{... | collective-permute-start | bytes 2985992 | tf_op jit(solution)/shard_map/ppermute | solution.py:48
  327.0 25.9 %collective-permute-start.21 = (bf16[448,384]{1,0:T(8,128)(2,1)S(1)}, bf16[448,384]{1,0:T(8,128)(2,1)S(1)}, u32[]{:S(2)}, u32[]{:S(2)}) collective-permute-start(bf16[448,384]{1,0:T(8,128)(2,1)S(1)} %fusion.55), channel_id=1, source_target_pairs={{0,16},{4,20},{8,24},{12,28},{16,0},{20,4},{24,8},{28,12},{1,17},{... | collective-permute-start | bytes 1032200 | tf_op jit(solution)/shard_map/ppermute | solution.py:48
  348.9 13.3 %collective-permute-start.15 = (bf16[648,384]{1,0:T(8,128)(2,1)}, bf16[648,384]{1,0:T(8,128)(2,1)}, u32[]{:S(2)}, u32[]{:S(2)}) collective-permute-start(bf16[648,384]{1,0:T(8,128)(2,1)} %fusion.40), channel_id=1, source_target_pairs={{0,16},{4,20},{8,24},{12,28},{16,0},{20,4},{24,8},{28,12},{1,17},{... | collective-permute-start | bytes 1493000 | tf_op jit(solution)/shard_map/ppermute | solution.py:48
  352.1 13.6 %collective-permute-start.17 = (bf16[648,384]{1,0:T(8,128)(2,1)}, bf16[648,384]{1,0:T(8,128)(2,1)}, u32[]{:S(2)}, u32[]{:S(2)}) collective-permute-start(bf16[648,384]{1,0:T(8,128)(2,1)} %fusion.41), channel_id=1, source_target_pairs={{0,8},{4,12},{8,0},{12,4},{16,24},{20,28},{24,16},{28,20},{1,9},{5... | collective-permute-start | bytes 1493000 | tf_op jit(solution)/shard_map/ppermute | solution.py:48
  353.2 25.8 %collective-permute-start.22 = (bf16[2,109,384]{2,1,0:T(8,128)(2,1)S(1)}, bf16[2,109,384]{2,1,0:T(8,128)(2,1)S(1)}, u32[]{:S(2)}, u32[]{:S(2)}) collective-permute-start(bf16[2,109,384]{2,1,0:T(8,128)(2,1)S(1)} %fusion.82), channel_id=1, source_target_pairs={{0,1},{1,0},{2,3},{3,2},{4,5},{5,4},{6,7},{7,6},{8,9},{9,8},{10,11... | collective-permute-start | bytes 502280 | tf_op jit(solution)/shard_map/ppermute | solution.py:48
  369.7 14.4 %collective-permute-start.18 = (bf16[2,324,384]{2,1,0:T(8,128)(2,1)S(1)}, bf16[2,324,384]{2,1,0:T(8,128)(2,1)S(1)}, u32[]{:S(2)}, u32[]{:S(2)}) collective-permute-start(bf16[2,324,384]{2,1,0:T(8,128)(2,1)S(1)} %fusion.39), channel_id=1, source_target_pairs={{0,1},{1,0},{2,3},{3,2},{4,5},{5,4},{6,7},{7,6},{8,9},{9,8},{10,11... | collective-permute-start | bytes 1493000 | tf_op jit(solution)/shard_map/ppermute | solution.py:48
  379.1 9.7 %collective-permute-start.23 = (bf16[109,384]{1,0:T(8,128)(2,1)S(1)}, bf16[109,384]{1,0:T(8,128)(2,1)S(1)}, u32[]{:S(2)}, u32[]{:S(2)}) collective-permute-start(bf16[109,384]{1,0:T(8,128)(2,1)S(1)} %fusion.85), channel_id=1, source_target_pairs={{0,2},{1,3},{2,0},{3,1},{4,6},{5,7},{6,4},{7,5},{8,10},{9,11},{10,... | collective-permute-start | bytes 251144 | tf_op jit(solution)/shard_map/ppermute | solution.py:48
  384.2 12.6 %collective-permute-start.19 = (bf16[324,384]{1,0:T(8,128)(2,1)S(1)}, bf16[324,384]{1,0:T(8,128)(2,1)S(1)}, u32[]{:S(2)}, u32[]{:S(2)}) collective-permute-start(bf16[324,384]{1,0:T(8,128)(2,1)S(1)} %fusion.81), channel_id=1, source_target_pairs={{0,2},{1,3},{2,0},{3,1},{4,6},{5,7},{6,4},{7,5},{8,10},{9,11},{10,... | collective-permute-start | bytes 746504 | tf_op jit(solution)/shard_map/ppermute | solution.py:48
  (42 other events, 222.8 us)
Sparse Core Ops, SparseCore 0:
  11.4 60.9 all-gather.4
  75.2 74.9 all-gather.6

commit v3 on v2

--- a/solution.py
+++ b/solution.py
@@ -168,8 +168,14 @@
     part = local_first.shape[0] // n_ha
     big = local_first.reshape((2,) * len(ha_bits) + (part, channels))
     big = halve(big, "ha", [0], ha_bits[::-1])
+    grad_wide = with_halo(
+        grad_hidden.reshape(frames, plane, channels)[:, :cells].reshape(
+            frames, height, breadth, channels
+        ),
+        sides,
+    )
     left = ha_bits[:0:-1]
-    first, big, small = lax.optimization_barrier((first, big, small))
+    grad_wide, big, small = lax.optimization_barrier((grad_wide, big, small))
     small = halve(small, "ha", ha_bits[1:], left)
     ups = small[:up_part].reshape(n_wa, up_rows, channels)
     small = jnp.concatenate([ups, small[up_part : up_part + n_wa][:, None]], axis=1)
@@ -185,22 +191,22 @@
     big = jnp.stack(ends).reshape((2,) * len(wa_bits) + (part // n_wa, channels))
     conv_grad = halve(big, "wa", wa_bits, wa_bits[::-1])
 
-    grad_wide = with_halo(
-        grad_hidden.reshape(frames, plane, channels)[:, :cells].reshape(
-            frames, height, breadth, channels
-        ),
-        sides,
-    )
-    grad_taps = spatial_taps(grad_wide, height, breadth, plane, True)
-    grad_taps = jnp.pad(grad_taps, ((2, 2), (0, 0), (0, 0))).reshape((frames + 4) * plane, size)
-    turned = jnp.swapaxes(first.reshape(3, 9, channels, channels), 2, 3).reshape(3, size, channels)
+    blocks = first.reshape(27, channels, channels)
     long = (frames + 2) * plane
     feature = jnp.zeros((long, channels), f32)
-    for a in range(3):
-        start = (2 - a) * plane
-        feature = feature + jnp.dot(
-            grad_taps[start : start + long], turned[a], preferred_element_type=f32
-        )
+    for row_tap in range(3):
+        for col_tap in range(3):
+            b, c = 2 - row_tap, 2 - col_tap
+            piece = flat_cells(grad_wide[:, b : b + height, c : c + breadth], plane)
+            piece = jnp.pad(piece, ((2, 2), (0, 0), (0, 0))).reshape(-1, channels)
+            for a in range(3):
+                start = (2 - a) * plane
+                feature = feature + lax.dot_general(
+                    piece[start : start + long],
+                    blocks[(a * 3 + row_tap) * 3 + col_tap],
+                    (((1,), (1,)), ((), ())),
+                    preferred_element_type=f32,
+                )
     feature_grad = (
         feature.astype(bf16)
         .reshape(frames + 2, plane, channels)[:, :cells]

time: 410 us -> 419 us (1.022)
    reshape x1 -> x0, local copies, waits for them, and re-layouts: 12.9 us -> none  [body(): first.reshape(3, 9, channels, channels)]
    reshape x8 -> x9, local copies, waits for them, and re-layouts: 5.31 us -> 15.6 us  [flat_cells(): cells = window.reshape(frames, height * breadth, channels)]
    slice x2 -> x10, local copies, waits for them, and re-layouts: 13.6 us -> 23.9 us  [the longest x9 21.8 us: body(): piece[start:start + long]]
    dot_general x3 -> x27, matrix products: 15.2 us -> 25.2 us  [body(): lax.dot_general(piece[start:start + long], blocks[(a * 3 + row_tap) * 3 +...]
    optimization_barrier x1 -> x0, local copies, waits for them, and re-layouts: 9.31 us -> none  [body(): first, big, small = lax.optimization_barrier((first, big, small))]
    unnamed x108 -> x125, local copies, waits for them, and re-layouts: 26.2 us -> 31.3 us
    concatenate x5 -> x4, other arithmetic: 11.5 us -> 6.54 us  [with_halo(): block = jnp.concatenate([low, block, high], axis=dim)]
    unnamed x14 -> x11, other arithmetic: 8.52 us -> 8.3 us
  transfers between devices with their start and end apart: 26 -> 26, of which waited for: 8 -> 9; matrix products, arithmetic and copies ran while one was open for 42% -> 31% of each run, Pallas kernels for 0% -> 0%
where the time goes in v3:
time: 419 us; the launch traced here: 413 us
  local copies, waits for them, and re-layouts  130 us (31%)
  waiting for transfers between devices  87.3 us (21%)
  other arithmetic  70.5 us (17%)
  matrix products  58.4 us (14%)
  starting transfers between devices  51.2 us (12%)
  between operations  15.9 us (4%)
    ppermute x12, waiting for transfers between devices, halve(): lax.ppermute(send.astype(jnp.bfloat16), axis, [(i, i ^ 1 << bit) for i in...  40.1 us
    all_gather x1, waiting for transfers between devices, body(): first = lax.all_gather(conv_weight, ('ha', 'wa'), axis=0, tiled=True)  38.4 us
    unnamed x125, local copies, waits for them, and re-layouts  31.3 us
    dot_general x27, matrix products, body(): lax.dot_general(piece[start:start + long], blocks[(a * 3 + row_tap) * 3 +...  25.2 us
    concatenate x1, other arithmetic, body(): jnp.concatenate([(lax.dot_general(taps[a * plane:a * plane + length], gra...  24 us
    ppermute x6, starting transfers between devices, with_halo(): lax.ppermute(lax.slice_in_dim(block, block.shape[dim] - 1, None, axis=dim...  23.4 us
    slice x9, local copies, waits for them, and re-layouts, body(): piece[start:start + long]  21.8 us
    ppermute x12, starting transfers between devices, halve(): lax.ppermute(send.astype(jnp.bfloat16), axis, [(i, i ^ 1 << bit) for i in...  20 us
  transfers between devices with their start and end apart: 26, of which 9 were waited for; matrix products, arithmetic and copies ran while one was open for 31% of the time, Pallas kernels for 0%

profile of v3, /device:TPU:0, one launch (start us, length us, event | category | flops | bytes accessed | tf_op | source)
XLA Modules:
  0.0 413.4 jit_solution(11642693423370102861)
XLA Ops:
  14.2 4.0 collective-permute-done.1
  21.6 4.5 %collective-permute-start.2 = (bf16[7,7,1,384]{3,0,2,1:T(8,128)(2,1)S(1)}, bf16[7,7,1,384]{3,0,2,1:T(8,128)(2,1)S(1)}, u32[]{:S(2)}, u32[]{:S(2)}) collective-permute-start(bf16[7,7,1,384]{3,0,2,1:T(8,128)(2,1)S(1)} %get-tuple-element.59), channel_id=1, source_target_pairs={{0,1},{1,2},{2,3},{4,5},{5,6},{6,7},{8,9},{9,10},{10,11},{12,13},{... | collective-permute-start | bytes 112904 | tf_op jit(solution)/shard_map/ppermute | solution.py:16
  27.2 4.8 %collective-permute-start.4 = (bf16[5,1,40,384]{3,2,1,0:T(8,128)(2,1)S(1)}, bf16[5,1,40,384]{3,2,1,0:T(8,128)(2,1)S(1)}, u32[]{:S(2)}, u32[]{:S(2)}) collective-permute-start(bf16[5,1,40,384]{3,2,1,0:T(8,128)(2,1)S(1)} %get-tuple-element.48), channel_id=1, source_target_pairs={{0,4},{4,8},{8,12},{12,16},{16,20},{20,24},{24,28},{1,5},{5,9},{9,... | collective-permute-start | bytes 460808 | tf_op jit(solution)/shard_map/ppermute | solution.py:16
  39.3 4.8 %collective-permute-start.6 = (bf16[5,12,1,384]{3,2,1,0:T(2,128)(2,1)S(1)}, bf16[5,12,1,384]{3,2,1,0:T(2,128)(2,1)S(1)}, u32[]{:S(2)}, u32[]{:S(2)}) collective-permute-start(bf16[5,12,1,384]{3,2,1,0:T(2,128)(2,1)S(1)} %get-tuple-element.37), channel_id=1, source_target_pairs={{0,1},{1,2},{2,3},{4,5},{5,6},{6,7},{8,9},{9,10},{10,11},{12,13},{... | collective-permute-start | bytes 138248 | tf_op jit(solution)/shard_map/ppermute | solution.py:16
  86.3 4.5 %slice_convert_fusion = f32[32,108,384]{2,1,0:T(8,128)} fusion(bf16[32,112,384]{2,1,0:T(8,128)(2,1)} %bitcast.213), kind=kLoop, calls=%fused_computation.12 | loop fusion | flops 1327104 | bytes 7962624 | tf_op jit(solution)/shard_map/transpose | solution.py:89
  90.8 5.5 %reshape.384 = f32[3,3,384,384]{3,2,1,0:T(8,128)} reshape(f32[32,108,384]{2,1,0:T(8,128)} %slice_convert_fusion) | data formatting | bytes 10616832 | tf_op jit(solution)/shard_map/transpose | solution.py:89
  105.2 6.6 %copy.38 = bf16[4,4,384,384]{3,2,1,0:T(8,128)(2,1)} copy(bf16[4,4,384,384]{2,3,1,0:T(8,128)(2,1)} %pad_maximum_fusion.1) | data formatting | bytes 9437184 | tf_op jit(solution)/shard_map/stack | solution.py:94
  111.8 38.4 %all-gather.7.cloned.1.call-done = bf16[32,324,384]{2,1,0:T(8,128)(2,1)} async-done(((bf16[1,324,384]{2,1,0:T(8,128)(2,1)}), bf16[32,324,384]{2,1,0:T(8,128)(2,1)}) %all-gather.7.cloned.1.call-update) | async-done | bytes 7962640 | tf_op jit(solution)/shard_map/all_gather | solution.py:79
  150.3 9.6 %reshape.387 = bf16[10368,384]{1,0:T(8,128)(2,1)} reshape(bf16[32,324,384]{2,1,0:T(8,128)(2,1)} %all-gather.7.cloned.1.call-done) | data formatting | bytes 15925248
  159.9 5.3 %fusion.3 = f32[560,384]{1,0:T(8,128)S(1)} fusion(bf16[560,3456]{1,0:T(8,128)(2,1)} %bitcast.204, bf16[10368,384]{1,0:T(8,128)(2,1)} %reshape.387), kind=kOutput, calls=%fused_computation.14 | convolution fusion | flops 1486356480 | bytes 7385088 | tf_op jit(solution)/shard_map/dot_general | solution.py:105
  170.8 7.2 %multiply_reduce_fusion = (f32[384]{0:T(512)S(1)}, f32[560]{0:T(1024)S(1)}, f32[560,384]{1,0:T(8,128)S(1)}) fusion(f32[560,384]{1,0:T(8,128)S(1)} %get-tuple-element.106, f32[560]{0:T(1024)S(1)} %add_rsqrt_fusion, f32[384]{0:T(512)S(1)} %reshape.373, bf16[560,6144]{1,0:T(8,128)(2,1)} %bitcast.13, bf16[6144,384]{1,0:T(8,128)(2,1)S(1)} %bitcast.203), kind=kOutput, calls=%fused_computation.111 | convolution fusion | flops 2645851136 | bytes 13327744 | tf_op jit(solution)/shard_map/dot_general | solution.py:95
  178.3 3.1 fusion.2
  181.5 3.1 fusion.1
  184.6 3.1 fusion
  187.8 6.7 %fusion.42 = f32[384,6144]{1,0:T(8,128)S(1)} fusion(bf16[560,6144]{1,0:T(8,128)(2,1)} %bitcast.13, f32[560,384]{1,0:T(8,128)S(1)} %get-tuple-element.106, f32[384]{0:T(512)S(1)} %reshape.373, f32[560]{0:T(1024)S(1)} %add_rsqrt_fusion), kind=kOutput, calls=%fused_computation.195 | convolution fusion | flops 2643916800 | bytes 17182400 | tf_op jit(solution)/shard_map/dot_general | solution.py:137
  194.5 24.0 %pad_maximum_fusion = bf16[10368,384]{1,0:T(8,128)(2,1)S(1)} fusion(bf16[3456,384]{1,0:T(8,128)(2,1)S(1)} %fusion.2, bf16[3456,384]{1,0:T(8,128)(2,1)S(1)} %fusion.1, bf16[3456,384]{1,0:T(8,128)(2,1)S(1)} %fusion), kind=kLoop, calls=%fused_computation | loop fusion | flops 23887872 | bytes 15925248 | tf_op jit(solution)/shard_map/concatenate | solution.py:122
  242.3 4.8 %collective-permute-start.10 = (bf16[5,7,1,384]{3,2,1,0:T(2,128)(2,1)S(1)}, bf16[5,7,1,384]{3,2,1,0:T(2,128)(2,1)S(1)}, u32[]{:S(2)}, u32[]{:S(2)}) collective-permute-start(bf16[5,7,1,384]{3,2,1,0:T(2,128)(2,1)S(1)} %get-tuple-element.69), channel_id=1, source_target_pairs={{0,1},{1,2},{2,3},{4,5},{5,6},{6,7},{8,9},{9,10},{10,11},{12,13},{... | collective-permute-start | bytes 80648 | tf_op jit(solution)/shard_map/ppermute | solution.py:16
  252.2 7.3 %convert_add_fusion = f32[2,2,1296,384]{3,2,1,0:T(8,128)} fusion(bf16[2,2,1296,384]{3,2,1,0:T(8,128)(2,1)} %collective-permute-done.12, bf16[2,2,2,1296,384]{4,3,2,1,0:T(8,128)(2,1)} %bitcast.200, s32[]{:T(128)S(6)} %select_n.55), kind=kLoop, calls=%fused_computation.1 | loop fusion | flops 5971968 | bytes 15925252 | tf_op jit(solution)/shard_map/add | solution.py:51
  300.6 3.9 fusion.111
  333.5 11.1 %collective-permute-done.20 = bf16[2,448,384]{2,1,0:T(8,128)(2,1)S(1)} collective-permute-done((bf16[2,448,384]{2,1,0:T(8,128)(2,1)S(1)}, bf16[2,448,384]{2,1,0:T(8,128)(2,1)S(1)}, u32[]{:S(2)}, u32[]{:S(2)}) %collective-permute-start.20) | collective-permute-done | bytes 688160 | tf_op jit(solution)/shard_map/ppermute | solution.py:48
  351.4 4.2 %collective-permute-done.21 = bf16[448,384]{1,0:T(8,128)(2,1)S(1)} collective-permute-done((bf16[448,384]{1,0:T(8,128)(2,1)S(1)}, bf16[448,384]{1,0:T(8,128)(2,1)S(1)}, u32[]{:S(2)}, u32[]{:S(2)}) %collective-permute-start.21) | collective-permute-done | bytes 344096 | tf_op jit(solution)/shard_map/ppermute | solution.py:48
  359.3 6.8 %collective-permute-done.15 = bf16[648,384]{1,0:T(8,128)(2,1)} collective-permute-done((bf16[648,384]{1,0:T(8,128)(2,1)}, bf16[648,384]{1,0:T(8,128)(2,1)}, u32[]{:S(2)}, u32[]{:S(2)}) %collective-permute-start.15) | collective-permute-done | bytes 497696 | tf_op jit(solution)/shard_map/ppermute | solution.py:48
  384.7 7.3 %collective-permute-done.18 = bf16[2,324,384]{2,1,0:T(8,128)(2,1)S(1)} collective-permute-done((bf16[2,324,384]{2,1,0:T(8,128)(2,1)S(1)}, bf16[2,324,384]{2,1,0:T(8,128)(2,1)S(1)}, u32[]{:S(2)}, u32[]{:S(2)}) %collective-permute-start.18) | collective-permute-done | bytes 497696 | tf_op jit(solution)/shard_map/ppermute | solution.py:48
  394.6 10.7 %collective-permute-done.19 = bf16[324,384]{1,0:T(8,128)(2,1)S(1)} collective-permute-done((bf16[324,384]{1,0:T(8,128)(2,1)S(1)}, bf16[324,384]{1,0:T(8,128)(2,1)S(1)}, u32[]{:S(2)}, u32[]{:S(2)}) %collective-permute-start.19) | collective-permute-done | bytes 248864 | tf_op jit(solution)/shard_map/ppermute | solution.py:48
  (310 shorter events, 206.2 us)
Async XLA Ops:
  7.2 78.2 %all-gather.5.cloned.1.call-start = ((), (), s32[]{:S(2)}) async-start(), calls=%async_computation | async-start | bytes 2838528 | tf_op jit(solution)/shard_map/all_gather | solution.py:74
  8.8 141.5 %all-gather.7.cloned.1.call-start = ((), (), s32[]{:S(2)}) async-start(), calls=%async_computation.1 | async-start | bytes 8312832 | tf_op jit(solution)/shard_map/all_gather | solution.py:79
  12.9 5.3 %collective-permute-start.1 = (bf16[7,1,20,384]{3,0,2,1:T(8,128)(2,1)S(1)}, bf16[7,1,20,384]{3,0,2,1:T(8,128)(2,1)S(1)}, u32[]{:S(2)}, u32[]{:S(2)}) collective-permute-start(bf16[7,1,20,384]{3,0,2,1:T(8,128)(2,1)S(1)} %get-tuple-element.74), channel_id=1, source_target_pairs={{4,0},{8,4},{12,8},{16,12},{20,16},{24,20},{28,24},{5,1},{9,5},{13... | collective-permute-start | bytes 322568 | tf_op jit(solution)/shard_map/ppermute | solution.py:19
  20.3 13.0 %collective-permute-start.3 = (bf16[7,7,1,384]{3,0,2,1:T(8,128)(2,1)S(1)}, bf16[7,7,1,384]{3,0,2,1:T(8,128)(2,1)S(1)}, u32[]{:S(2)}, u32[]{:S(2)}) collective-permute-start(bf16[7,7,1,384]{3,0,2,1:T(8,128)(2,1)S(1)} %get-tuple-element.58), channel_id=1, source_target_pairs={{1,0},{2,1},{3,2},{5,4},{6,5},{7,6},{9,8},{10,9},{11,10},{13,12},{... | collective-permute-start | bytes 112904 | tf_op jit(solution)/shard_map/ppermute | solution.py:19
  21.6 11.7 %collective-permute-start.2 = (bf16[7,7,1,384]{3,0,2,1:T(8,128)(2,1)S(1)}, bf16[7,7,1,384]{3,0,2,1:T(8,128)(2,1)S(1)}, u32[]{:S(2)}, u32[]{:S(2)}) collective-permute-start(bf16[7,7,1,384]{3,0,2,1:T(8,128)(2,1)S(1)} %get-tuple-element.59), channel_id=1, source_target_pairs={{0,1},{1,2},{2,3},{4,5},{5,6},{6,7},{8,9},{9,10},{10,11},{12,13},{... | collective-permute-start | bytes 112904 | tf_op jit(solution)/shard_map/ppermute | solution.py:16
  27.2 9.6 %collective-permute-start.4 = (bf16[5,1,40,384]{3,2,1,0:T(8,128)(2,1)S(1)}, bf16[5,1,40,384]{3,2,1,0:T(8,128)(2,1)S(1)}, u32[]{:S(2)}, u32[]{:S(2)}) collective-permute-start(bf16[5,1,40,384]{3,2,1,0:T(8,128)(2,1)S(1)} %get-tuple-element.48), channel_id=1, source_target_pairs={{0,4},{4,8},{8,12},{12,16},{16,20},{20,24},{24,28},{1,5},{5,9},{9,... | collective-permute-start | bytes 460808 | tf_op jit(solution)/shard_map/ppermute | solution.py:16
  32.0 5.7 %collective-permute-start.5 = (bf16[5,1,40,384]{3,2,1,0:T(8,128)(2,1)S(1)}, bf16[5,1,40,384]{3,2,1,0:T(8,128)(2,1)S(1)}, u32[]{:S(2)}, u32[]{:S(2)}) collective-permute-start(bf16[5,1,40,384]{3,2,1,0:T(8,128)(2,1)S(1)} %get-tuple-element.47), channel_id=1, source_target_pairs={{4,0},{8,4},{12,8},{16,12},{20,16},{24,20},{28,24},{5,1},{9,5},{13... | collective-permute-start | bytes 460808 | tf_op jit(solution)/shard_map/ppermute | solution.py:19
  38.0 16.0 %collective-permute-start.7 = (bf16[5,12,1,384]{3,2,1,0:T(2,128)(2,1)S(1)}, bf16[5,12,1,384]{3,2,1,0:T(2,128)(2,1)S(1)}, u32[]{:S(2)}, u32[]{:S(2)}) collective-permute-start(bf16[5,12,1,384]{3,2,1,0:T(2,128)(2,1)S(1)} %get-tuple-element.38), channel_id=1, source_target_pairs={{1,0},{2,1},{3,2},{5,4},{6,5},{7,6},{9,8},{10,9},{11,10},{13,12},{... | collective-permute-start | bytes 138248 | tf_op jit(solution)/shard_map/ppermute | solution.py:19
  39.3 14.7 %collective-permute-start.6 = (bf16[5,12,1,384]{3,2,1,0:T(2,128)(2,1)S(1)}, bf16[5,12,1,384]{3,2,1,0:T(2,128)(2,1)S(1)}, u32[]{:S(2)}, u32[]{:S(2)}) collective-permute-start(bf16[5,12,1,384]{3,2,1,0:T(2,128)(2,1)S(1)} %get-tuple-element.37), channel_id=1, source_target_pairs={{0,1},{1,2},{2,3},{4,5},{5,6},{6,7},{8,9},{9,10},{10,11},{12,13},{... | collective-permute-start | bytes 138248 | tf_op jit(solution)/shard_map/ppermute | solution.py:16
  222.8 29.4 %collective-permute-start.12 = (bf16[2,2,1296,384]{3,2,1,0:T(8,128)(2,1)}, bf16[2,2,1296,384]{3,2,1,0:T(8,128)(2,1)}, u32[]{:S(2)}, u32[]{:S(2)}) collective-permute-start(bf16[2,2,1296,384]{3,2,1,0:T(8,128)(2,1)} %dynamic-slice_bitcast_fusion), channel_id=1, source_target_pairs={{0,4},{4,0},{8,12},{12,8},{16,20},{20,16},{24,28},{28,24},{1,5},{5... | collective-permute-start | bytes 11943944 | tf_op jit(solution)/shard_map/ppermute | solution.py:48
  234.4 14.7 %collective-permute-start.13 = (bf16[2,2,448,384]{3,2,0,1:T(8,128)(2,1)}, bf16[2,2,448,384]{3,2,0,1:T(8,128)(2,1)S(1)}, u32[]{:S(2)}, u32[]{:S(2)}) collective-permute-start(bf16[2,2,448,384]{3,2,0,1:T(8,128)(2,1)} %bitcast.190), channel_id=1, source_target_pairs={{0,4},{4,0},{8,12},{12,8},{16,20},{20,16},{24,28},{28,24},{1,5},{5... | collective-permute-start | bytes 4128776 | tf_op jit(solution)/shard_map/ppermute | solution.py:48
  237.0 3.9 collective-permute-start.9
  241.0 6.1 %collective-permute-start.11 = (bf16[5,7,1,384]{3,2,1,0:T(2,128)(2,1)S(1)}, bf16[5,7,1,384]{3,2,1,0:T(2,128)(2,1)S(1)}, u32[]{:S(2)}, u32[]{:S(2)}) collective-permute-start(bf16[5,7,1,384]{3,2,1,0:T(2,128)(2,1)S(1)} %get-tuple-element.70), channel_id=1, source_target_pairs={{1,0},{2,1},{3,2},{5,4},{6,5},{7,6},{9,8},{10,9},{11,10},{13,12},{... | collective-permute-start | bytes 80648 | tf_op jit(solution)/shard_map/ppermute | solution.py:19
  242.3 6.3 %collective-permute-start.10 = (bf16[5,7,1,384]{3,2,1,0:T(2,128)(2,1)S(1)}, bf16[5,7,1,384]{3,2,1,0:T(2,128)(2,1)S(1)}, u32[]{:S(2)}, u32[]{:S(2)}) collective-permute-start(bf16[5,7,1,384]{3,2,1,0:T(2,128)(2,1)S(1)} %get-tuple-element.69), channel_id=1, source_target_pairs={{0,1},{1,2},{2,3},{4,5},{5,6},{6,7},{8,9},{9,10},{10,11},{12,13},{... | collective-permute-start | bytes 80648 | tf_op jit(solution)/shard_map/ppermute | solution.py:16
  304.6 41.7 %collective-permute-start.14 = (bf16[2,648,384]{2,1,0:T(8,128)(2,1)S(1)}, bf16[2,648,384]{2,1,0:T(8,128)(2,1)S(1)}, u32[]{:S(2)}, u32[]{:S(2)}) collective-permute-start(bf16[2,648,384]{2,1,0:T(8,128)(2,1)S(1)} %fusion.19), channel_id=1, source_target_pairs={{0,8},{4,12},{8,0},{12,4},{16,24},{20,28},{24,16},{28,20},{1,9},{5... | collective-permute-start | bytes 2985992 | tf_op jit(solution)/shard_map/ppermute | solution.py:48
  307.8 40.2 %collective-permute-start.16 = (bf16[2,648,384]{2,1,0:T(8,128)(2,1)S(1)}, bf16[2,648,384]{2,1,0:T(8,128)(2,1)S(1)}, u32[]{:S(2)}, u32[]{:S(2)}) collective-permute-start(bf16[2,648,384]{2,1,0:T(8,128)(2,1)S(1)} %fusion.20), channel_id=1, source_target_pairs={{0,16},{4,20},{8,24},{12,28},{16,0},{20,4},{24,8},{28,12},{1,17},{... | collective-permute-start | bytes 2985992 | tf_op jit(solution)/shard_map/ppermute | solution.py:48
  308.9 35.6 %collective-permute-start.20 = (bf16[2,448,384]{2,1,0:T(8,128)(2,1)S(1)}, bf16[2,448,384]{2,1,0:T(8,128)(2,1)S(1)}, u32[]{:S(2)}, u32[]{:S(2)}) collective-permute-start(bf16[2,448,384]{2,1,0:T(8,128)(2,1)S(1)} %fusion.21), channel_id=1, source_target_pairs={{0,8},{4,12},{8,0},{12,4},{16,24},{20,28},{24,16},{28,20},{1,9},{5... | collective-permute-start | bytes 2064392 | tf_op jit(solution)/shard_map/ppermute | solution.py:48
  344.7 10.9 %collective-permute-start.21 = (bf16[448,384]{1,0:T(8,128)(2,1)S(1)}, bf16[448,384]{1,0:T(8,128)(2,1)S(1)}, u32[]{:S(2)}, u32[]{:S(2)}) collective-permute-start(bf16[448,384]{1,0:T(8,128)(2,1)S(1)} %fusion.51), channel_id=1, source_target_pairs={{0,16},{4,20},{8,24},{12,28},{16,0},{20,4},{24,8},{28,12},{1,17},{... | collective-permute-start | bytes 1032200 | tf_op jit(solution)/shard_map/ppermute | solution.py:48
  347.4 18.7 %collective-permute-start.15 = (bf16[648,384]{1,0:T(8,128)(2,1)}, bf16[648,384]{1,0:T(8,128)(2,1)}, u32[]{:S(2)}, u32[]{:S(2)}) collective-permute-start(bf16[648,384]{1,0:T(8,128)(2,1)} %fusion.40), channel_id=1, source_target_pairs={{0,16},{4,20},{8,24},{12,28},{16,0},{20,4},{24,8},{28,12},{1,17},{... | collective-permute-start | bytes 1493000 | tf_op jit(solution)/shard_map/ppermute | solution.py:48
  349.1 21.4 %collective-permute-start.17 = (bf16[648,384]{1,0:T(8,128)(2,1)}, bf16[648,384]{1,0:T(8,128)(2,1)}, u32[]{:S(2)}, u32[]{:S(2)}) collective-permute-start(bf16[648,384]{1,0:T(8,128)(2,1)} %fusion.41), channel_id=1, source_target_pairs={{0,8},{4,12},{8,0},{12,4},{16,24},{20,28},{24,16},{28,20},{1,9},{5... | collective-permute-start | bytes 1493000 | tf_op jit(solution)/shard_map/ppermute | solution.py:48
  356.6 25.2 %collective-permute-start.22 = (bf16[2,109,384]{2,1,0:T(8,128)(2,1)}, bf16[2,109,384]{2,1,0:T(8,128)(2,1)}, u32[]{:S(2)}, u32[]{:S(2)}) collective-permute-start(bf16[2,109,384]{2,1,0:T(8,128)(2,1)} %fusion.106), channel_id=1, source_target_pairs={{0,1},{1,0},{2,3},{3,2},{4,5},{5,4},{6,7},{7,6},{8,9},{9,8},{10,11... | collective-permute-start | bytes 502280 | tf_op jit(solution)/shard_map/ppermute | solution.py:48
  376.7 15.3 %collective-permute-start.18 = (bf16[2,324,384]{2,1,0:T(8,128)(2,1)S(1)}, bf16[2,324,384]{2,1,0:T(8,128)(2,1)S(1)}, u32[]{:S(2)}, u32[]{:S(2)}) collective-permute-start(bf16[2,324,384]{2,1,0:T(8,128)(2,1)S(1)} %fusion.39), channel_id=1, source_target_pairs={{0,1},{1,0},{2,3},{3,2},{4,5},{5,4},{6,7},{7,6},{8,9},{9,8},{10,11... | collective-permute-start | bytes 1493000 | tf_op jit(solution)/shard_map/ppermute | solution.py:48
  382.8 11.2 %collective-permute-start.23 = (bf16[109,384]{1,0:T(8,128)(2,1)S(1)}, bf16[109,384]{1,0:T(8,128)(2,1)S(1)}, u32[]{:S(2)}, u32[]{:S(2)}) collective-permute-start(bf16[109,384]{1,0:T(8,128)(2,1)S(1)} %fusion.109), channel_id=1, source_target_pairs={{0,2},{1,3},{2,0},{3,1},{4,6},{5,7},{6,4},{7,5},{8,10},{9,11},{10,... | collective-permute-start | bytes 251144 | tf_op jit(solution)/shard_map/ppermute | solution.py:48
  392.2 13.1 %collective-permute-start.19 = (bf16[324,384]{1,0:T(8,128)(2,1)S(1)}, bf16[324,384]{1,0:T(8,128)(2,1)S(1)}, u32[]{:S(2)}, u32[]{:S(2)}) collective-permute-start(bf16[324,384]{1,0:T(8,128)(2,1)S(1)} %fusion.105), channel_id=1, source_target_pairs={{0,2},{1,3},{2,0},{3,1},{4,6},{5,7},{6,4},{7,5},{8,10},{9,11},{10,... | collective-permute-start | bytes 746504 | tf_op jit(solution)/shard_map/ppermute | solution.py:48
  (53 other events, 229.2 us)
Sparse Core Ops, SparseCore 0:
  11.4 61.0 all-gather.4
  75.3 74.9 all-gather.6
